TPU v7x, 512 devices: a whole 4x4x16 slice. The times are simulated.
512 devices in a mesh: elem: 64 (over z, x), param: 8 (over y, core).
Axes of the slice: x: 4, y: 4, z: 16, core: 2. Of those that a mesh axis runs over, the one named last changes fastest.
Arguments:
- coords: bfloat16 [32, 300], P('param'), may hold values from -6 to 6
- basis_rows: bfloat16 [3, 300, 65536], P(None, None, 'elem'), may hold values from -0.375 to 0.375
- connectivity: int32 [65536, 8], P(('elem', 'param')), may hold values from 0 to 1279, as said below
- modulus: float32 [65536], P(('elem', 'param')), may hold values from 0.5 to 15
- stiffness: float32 [24, 24], replicated, may hold values from -1.25 to 1.25
Outputs:
- training: bfloat16 [32, 300, 65536], P(None, None, ('elem', 'param'))
- target: float32 [32, 300], replicated
Inputs may be any that keep to these rules, and one draw needn't show every extreme that they name: `connectivity`: A number c of 1024 or more names node c - 1024 of the next node block; the last block's next block is the first. An element's eight corner numbers lie among min(8, 256) consecutive numbers; where these lie in the block is not tied to the element's position.
All inputs are finite; a program needn't handle non-finite values.
Results may differ from a plain program's by a relative error of at most 0.0072.
Values may be sent and summed in bfloat16 or wider, within the bound.
No kernel may reach another device: no remote copies, remote signals or barrier semaphores. Data moves between devices by JAX's collectives and lax.ppermute only.
A program may use at most 64 MiB of HBM per device.

v0:
```python
import math

import jax
import jax.numpy as jnp
from jax import lax
from jax.sharding import Mesh
from jax.sharding import PartitionSpec as P

ELEM = ("elem_0", "elem_1")
PARAM = ("param_0", "param_1")
ELEM_PARAM = ("elem_0", "elem_1", "param_0", "param_1")


def passed_along(value, axis, by):
    peers = lax.axis_size(axis)
    return lax.ppermute(value, axis, [(i, (i + by) % peers) for i in range(peers)])


def laid_out(parts, dim):
    shape = list(parts.shape[1:])
    shape[dim] *= parts.shape[0]
    return jnp.moveaxis(parts, 0, dim).reshape(shape)


def copy_for_each(value, axis):
    peers = lax.axis_size(axis)
    return lax.all_to_all(
        jnp.broadcast_to(value[None], (peers, *value.shape)), axis, 0, 0, tiled=True
    )


def collect(value, axis, dim):
    return laid_out(copy_for_each(value, axis), dim)


def in_blocks(value, dim, peers):
    before, after = (value.shape[:dim], value.shape[dim + 1 :])
    return jnp.moveaxis(value.reshape(*before, peers, -1, *after), dim, 0)


def summed_on_arrival(value, axis, dim):
    parts = in_blocks(value, dim, lax.axis_size(axis))
    arrived = lax.all_to_all(parts, axis, split_axis=0, concat_axis=0, tiled=True)
    return arrived.sum(axis=0)


def sum_in_two_steps(value, axes, dim):
    far, near = axes
    parts = in_blocks(value, dim, lax.axis_size(far))
    nearer = summed_on_arrival(parts, near, dim + 1)
    arrived = lax.all_to_all(nearer, far, split_axis=0, concat_axis=0, tiled=True)
    return arrived.sum(axis=0)


def filled_up(lines, peers):
    spare = -len(lines) % peers
    return jnp.pad(lines, [(0, spare)] + [(0, 0)] * (lines.ndim - 1))


def gathered_by_axis(value, axes, dim):
    far, near = axes
    parts = copy_for_each(copy_for_each(value, far), near)
    return laid_out(parts.swapaxes(0, 1).reshape(-1, *value.shape), dim)


def total_of(value, axes):
    own = sum_in_two_steps(
        filled_up(value, lax.axis_size(axes[0]) * lax.axis_size(axes[1])), axes, 0
    )
    whole = gathered_by_axis(own, axes, 0)
    return whole[: len(value)].reshape(value.shape)


def together(arrays, axis):
    ends = [0]
    for a in arrays:
        ends.append(ends[-1] + a.size)
    running = total_of(jnp.concatenate([a.ravel() for a in arrays]), axis)
    return tuple((running[b:e].reshape(a.shape) for a, b, e in zip(arrays, ends, ends[1:])))


def local(coords, basis_rows, connectivity, modulus, stiffness):
    node_count = basis_rows.shape[2]
    ghost_count = node_count // 4
    ghost_rows = passed_along(basis_rows[:, :, :ghost_count], ELEM, -1)
    extended = jnp.concatenate([basis_rows, ghost_rows], axis=2)
    corner_ids = connectivity.T
    elem_count = corner_ids.shape[1]
    element_basis = extended[:, :, corner_ids]
    cycle_size = lax.axis_size(PARAM)
    all_coords = collect(coords, PARAM, 0)
    displaced = jnp.stack(
        [
            jnp.dot(all_coords, extended[component], preferred_element_type=jnp.float32)
            for component in range(3)
        ],
        axis=1,
    ).astype(jnp.bfloat16)
    snaps = displaced.shape[0]
    corner_disp = displaced[:, :, corner_ids].reshape(snaps, 24, elem_count).astype(jnp.float32)
    linear = jnp.einsum("kj,sje->ske", stiffness, corner_disp, precision=lax.Precision.HIGHEST)
    forces = (modulus * (linear + 0.25 * corner_disp * corner_disp * corner_disp)).astype(
        jnp.bfloat16
    )
    forces = forces.reshape(snaps, 3, 8, elem_count)
    matrix = jnp.einsum("cmae,scae->sme", element_basis, forces, preferred_element_type=jnp.float32)
    norm_sums = jnp.sum(jnp.sqrt(jnp.sum(matrix * matrix, axis=1)), axis=1)
    force_sums = jnp.sum(matrix, axis=2)
    norm_sums, force_sums = together(
        (norm_sums, force_sums), (("elem_0", "elem_1"), ("param_0", "param_1"))
    )
    elem_total = elem_count * lax.axis_size(ELEM) * cycle_size
    row_scale = norm_sums / elem_total
    target = force_sums / (row_scale[:, None] * math.sqrt(elem_total))
    training = (matrix / row_scale[:, None, None]).astype(jnp.bfloat16)
    return (training, target)


def solution(mesh):
    split = Mesh(mesh.devices.reshape(16, 4, 4, 2), ("elem_0", "elem_1", "param_0", "param_1"))
    return jax.shard_map(
        local,
        mesh=split,
        in_specs=(P(PARAM, None), P(None, None, ELEM), P(ELEM_PARAM, None), P(ELEM_PARAM), P()),
        out_specs=(P(None, None, ELEM_PARAM), P()),
        check_vma=False,
    )
```

profile of v0, /device:TPU:1, one launch (start us, length us, event | category | flops | bytes accessed | tf_op | source)
XLA Modules:
  0.0 168.4 jit_solution(12543320956963072040)
XLA Ops:
  0.6 1.8 %slice.21 = bf16[3,300,256]{2,1,0:T(8,128)(2,1)} slice(bf16[3,300,1024]{2,1,0:T(8,128)(2,1)} %param.6), slice={[0:3], [0:300], [0:256]} | slice | bytes 921600 | tf_op jit(solution)/shard_map/slice | solution.py:85
  2.5 14.1 %collective-permute-start = (bf16[3,300,256]{2,1,0:T(8,128)(2,1)}, bf16[3,300,256]{2,1,0:T(8,128)(2,1)}, u32[]{:S(2)}, u32[]{:S(2)}) collective-permute-start(bf16[3,300,256]{2,1,0:T(8,128)(2,1)} %slice.21), channel_id=1, source_target_pairs={{0,504},{8,0},{16,8},{24,16},{32,24},{40,32},{48,40},{56,48},{64,5... | collective-permute-start | bytes 1382408 | tf_op jit(solution)/shard_map/ppermute | solution.py:16
  16.6 1.3 broadcast_in_dim.10
  17.9 5.4 %all-to-all-start = ((bf16[8,4,300]{2,1,0:T(4,128)(2,1)}), bf16[8,4,300]{2,1,0:T(4,128)(2,1)S(1)}, u32[]{:S(2)}, u32[]{:S(2)}) async-start(bf16[8,4,300]{2,1,0:T(4,128)(2,1)} %broadcast_in_dim.10), calls=%async_computation | async-start | bytes 49152 | tf_op jit(solution)/shard_map/all_to_all | solution.py:27
  23.3 0.7 fusion.21
  24.0 4.8 %copy.41 = bf16[3,300,1024]{1,0,2:T(4,128)(2,1)S(1)} copy(bf16[3,300,1024]{2,1,0:T(8,128)(2,1)} %param.6) | data formatting | bytes 3686400 | tf_op args[1]
  28.8 0.6 reshape.34
  29.4 2.1 %copy.42 = bf16[3,300,256]{1,0,2:T(4,128)(2,1)} copy(bf16[3,300,256]{2,1,0:T(8,128)(2,1)} %collective-permute-done) | data formatting | bytes 921600 | tf_op jit(solution)/shard_map/ppermute | solution.py:16
  31.6 22.6 %fusion.8 = (bf16[1,300,1280]{1,0,2:T(2,128)(2,1)}, bf16[1,300,1280]{1,0,2:T(2,128)(2,1)}, bf16[1,300,1280]{1,0,2:T(2,128)(2,1)}) fusion(bf16[3,300,1024]{1,0,2:T(4,128)(2,1)S(1)} %copy.41, bf16[3,300,256]{1,0,2:T(4,128)(2,1)} %copy.42), kind=kLoop, calls=%fused_computation.23 | loop fusion | flops 1152000 | bytes 4608000 | tf_op jit(solution)/shard_map/concatenate | solution.py:86
  54.1 8.6 %pad_maximum_fusion = bf16[3,300,1280]{1,0,2:T(4,128)(2,1)} fusion(bf16[3,300,256]{1,0,2:T(4,128)(2,1)S(1)} %copy-done.2, bf16[3,300,1024]{1,0,2:T(4,128)(2,1)S(1)} %copy.41), kind=kLoop, calls=%fused_computation.10 | loop fusion | flops 1152000 | bytes 4608000 | tf_op jit(solution)/shard_map/concatenate | solution.py:86
  62.7 4.0 %copy.43 = bf16[1,300,1280]{2,1,0:T(8,128)(2,1)S(1)} copy(bf16[1,300,1280]{1,0,2:T(2,128)(2,1)} %get-tuple-element.14) | data formatting | bytes 1536000 | tf_op jit(solution)/shard_map/slice | solution.py:94
  66.7 3.8 %copy.44 = bf16[1,300,1280]{2,1,0:T(8,128)(2,1)S(1)} copy(bf16[1,300,1280]{1,0,2:T(2,128)(2,1)} %get-tuple-element.15) | data formatting | bytes 1536000 | tf_op jit(solution)/shard_map/slice | solution.py:94
  70.5 1.6 fusion.5
  72.2 1.6 fusion.6
  73.8 2.7 %copy.45 = bf16[1,300,1280]{2,1,0:T(8,128)(2,1)S(1)} copy(bf16[1,300,1280]{1,0,2:T(2,128)(2,1)S(1)} %copy-done.1) | data formatting | bytes 1536000 | tf_op jit(solution)/shard_map/slice | solution.py:94
  76.5 1.0 fusion.7
  77.6 0.8 copy.46
  78.4 3.6 %gather_fusion = bf16[1024,32,3]{1,2,0:T(4,128)(2,1)S(1)} fusion(bf16[32,3,1280]{0,1,2:T(4,128)(2,1)S(1)} %copy.46, s32[1024]{0:T(1024)S(1)} %fusion.21), kind=kCustom, calls=%fused_computation | custom fusion | bytes 397312 | tf_op jit(solution)/shard_map/gather | solution.py:100
  82.0 0.5 copy.47
  82.5 0.3 fusion.14
  82.8 1.3 copy.49
  84.1 6.7 %gather_fusion.1 = bf16[1024,3,300]{2,1,0:T(4,128)(2,1)S(1)} fusion(bf16[3,300,1280]{1,0,2:T(4,128)(2,1)} %pad_maximum_fusion, s32[1024]{0:T(1024)S(1)} %fusion.21), kind=kCustom, calls=%fused_computation.1 | custom fusion | bytes 3690496 | tf_op jit(solution)/shard_map/gather | solution.py:89
  90.9 6.2 %fusion = (f32[32,128]{0,1:T(8,128)S(1)}, f32[32,300]{1,0:T(8,128)S(1)}, f32[128,32,300,1]{2,1,3,0:T(8,128)}) fusion(bf16[32,3,8,128]{0,2,1,3:T(8,128)(2,1)} %copy.49, bf16[8,128,3,300]{3,2,1,0:T(4,128)(2,1)S(1)} %bitcast.81), kind=kOutput, calls=%fused_computation.5 | convolution fusion | flops 62655104 | bytes 7009792 | tf_op jit(solution)/shard_map/cmae,scae->sme/dot_general | solution.py:106
  97.1 0.1 reshape.37
  97.3 0.1 select_maximum_fusion
  97.3 0.2 reshape_reshape.6
  97.6 0.2 copy.50
  97.7 0.1 reshape.61
  97.9 9.3 %all_to_all.30 = f32[8,1,1216]{2,1,0:T(1,128)S(1)} all-to-all(f32[8,1,1216]{2,1,0:T(1,128)S(1)} %reshape.61), channel_id=1, replica_groups=mesh['elem_0'=16,'elem_1'=4,'param_0'=4,'param_1'=2] {'param_0','param_1'}, dimensions={0} | all-to-all | bytes 77824 | tf_op jit(solution)/shard_map/all_to_all | solution.py:43
  107.2 0.5 broadcast.34
  107.7 0.7 reduce.1
  108.5 0.1 reshape.62
  108.6 0.1 copy.51
  108.7 22.2 %all_to_all.31 = f32[64,1,19]{2,1,0:T(1,128)S(1)} all-to-all(f32[64,1,19]{2,1,0:T(1,128)S(1)} %copy.51), channel_id=1, replica_groups=mesh['elem_0'=16,'elem_1'=4,'param_0'=4,'param_1'=2] {'elem_0','elem_1'}, dimensions={0} | all-to-all | bytes 9728 | tf_op jit(solution)/shard_map/all_to_all | solution.py:51
  130.8 0.1 reduce_sum.49
  131.0 17.4 %all_to_all.32 = f32[64,1,19]{2,1,0:T(1,128)S(1)} all-to-all(f32[64,1,19]{2,1,0:T(1,128)S(1)} %broadcast_in_dim.12), channel_id=1, replica_groups=mesh['elem_0'=16,'elem_1'=4,'param_0'=4,'param_1'=2] {'elem_0','elem_1'}, dimensions={0} | all-to-all | bytes 9728 | tf_op jit(solution)/shard_map/all_to_all | solution.py:27
  148.3 0.1 copy.52
  148.4 0.1 reshape.63
  148.5 10.5 %all_to_all.33 = f32[8,1,1216]{2,1,0:T(1,128)S(1)} all-to-all(f32[8,1,1216]{2,1,0:T(1,128)S(1)} %reshape.63), channel_id=1, replica_groups=mesh['elem_0'=16,'elem_1'=4,'param_0'=4,'param_1'=2] {'param_0','param_1'}, dimensions={0} | all-to-all | bytes 77824 | tf_op jit(solution)/shard_map/all_to_all | solution.py:27
  159.0 0.7 reduce.2
  159.8 0.1 reshape.64
  159.8 0.2 copy.53
  160.0 0.2 reshape_reshape.7
  160.2 0.1 slice.38
  160.3 0.1 reshape.38
  160.5 3.6 %fusion.1 = bf16[32,300,128]{1,0,2:T(8,128)(2,1)S(1)} fusion(f32[128,32,300,1]{2,1,3,0:T(8,128)} %get-tuple-element.19, f32[32]{0:T(128)S(1)} %get-tuple-element.18), kind=kLoop, calls=%fused_computation.6 | loop fusion | flops 2457600 | bytes 7372928 | tf_op jit(solution)/shard_map/convert_element_type | solution.py:115
  164.1 3.6 %copy.54 = bf16[32,300,128]{2,0,1:T(8,128)(2,1)} copy(bf16[32,300,128]{1,0,2:T(8,128)(2,1)S(1)} %fusion.1) | data formatting | bytes 4915200
  167.7 0.7 broadcast_divide_fusion
  (21 shorter events, 0.2 us)
Async XLA Ops:
  0.6 81.9 %copy-start = (f32[24,24]{1,0:T(8,128)S(1)}, f32[24,24]{1,0:T(8,128)}, u32[]{:S(2)}) copy-start(f32[24,24]{1,0:T(8,128)} %param.9) | copy-start | bytes 6916
  2.5 27.0 %collective-permute-start = (bf16[3,300,256]{2,1,0:T(8,128)(2,1)}, bf16[3,300,256]{2,1,0:T(8,128)(2,1)}, u32[]{:S(2)}, u32[]{:S(2)}) collective-permute-start(bf16[3,300,256]{2,1,0:T(8,128)(2,1)} %slice.21), channel_id=1, source_target_pairs={{0,504},{8,0},{16,8},{24,16},{32,24},{40,32},{48,40},{56,48},{64,5... | collective-permute-start | bytes 1382408 | tf_op jit(solution)/shard_map/ppermute | solution.py:16
  17.9 10.9 %all-to-all-start = ((bf16[8,4,300]{2,1,0:T(4,128)(2,1)}), bf16[8,4,300]{2,1,0:T(4,128)(2,1)S(1)}, u32[]{:S(2)}, u32[]{:S(2)}) async-start(bf16[8,4,300]{2,1,0:T(4,128)(2,1)} %broadcast_in_dim.10), calls=%async_computation | async-start | bytes 49152 | tf_op jit(solution)/shard_map/all_to_all | solution.py:27
  31.5 22.6 %copy-start.2 = (bf16[3,300,256]{1,0,2:T(4,128)(2,1)S(1)}, bf16[3,300,256]{1,0,2:T(4,128)(2,1)}, u32[]{:S(2)}) copy-start(bf16[3,300,256]{1,0,2:T(4,128)(2,1)} %copy.42) | copy-start | bytes 1382404
  62.7 11.1 %copy-start.1 = (bf16[1,300,1280]{1,0,2:T(2,128)(2,1)S(1)}, bf16[1,300,1280]{1,0,2:T(2,128)(2,1)}, u32[]{:S(2)}) copy-start(bf16[1,300,1280]{1,0,2:T(2,128)(2,1)} %get-tuple-element.16) | copy-start | bytes 2304004
  73.8 3.7 %copy-start.3 = (bf16[32,1,1280]{2,0,1:T(8,128)(2,1)S(1)}, bf16[32,1,1280]{2,0,1:T(8,128)(2,1)}, u32[]{:S(2)}) copy-start(bf16[32,1,1280]{2,0,1:T(8,128)(2,1)} %fusion.5) | copy-start | bytes 245764
  73.8 3.7 %copy-start.4 = (bf16[32,1,1280]{2,0,1:T(8,128)(2,1)S(1)}, bf16[32,1,1280]{2,0,1:T(8,128)(2,1)}, u32[]{:S(2)}) copy-start(bf16[32,1,1280]{2,0,1:T(8,128)(2,1)} %fusion.6) | copy-start | bytes 245764
  73.8 8.7 %copy-start.5 = (f32[128]{0:T(128)S(1)}, f32[128]{0:T(128)}, u32[]{:S(2)}) copy-start(f32[128]{0:T(128)} %param.8) | copy-start | bytes 1540
where the time goes:
time: 169 us; the launch traced here: 168 us
  blocking collectives  59.4 us (35%)
  local copies, waits for them, and re-layouts  39.9 us (24%)
  other arithmetic  37.9 us (22%)
  starting transfers between devices  19.6 us (12%)
  matrix products  10.8 us (6%)
    concatenate x2, other arithmetic, local(): extended = jnp.concatenate([basis_rows, ghost_rows], axis=2)  31.1 us
    all_to_all x2, blocking collectives, copy_for_each(): lax.all_to_all(jnp.broadcast_to(value[None], (peers, *value.shape)), axis...  27.8 us
    all_to_all x1, blocking collectives, sum_in_two_steps(): lax.all_to_all(nearer, far, split_axis=0, concat_axis=0, tiled=True)  22.2 us
    ppermute x1, starting transfers between devices, passed_along(): lax.ppermute(value, axis, [(i, (i + by) % peers) for i in range(peers)])  14.1 us
    slice x3, local copies, waits for them, and re-layouts, local(): extended[component]  10.5 us
    all_to_all x1, blocking collectives, summed_on_arrival(): lax.all_to_all(parts, axis, split_axis=0, concat_axis=0, tiled=True)  9.35 us
    unnamed x19, local copies, waits for them, and re-layouts  8.77 us
    gather x1, local copies, waits for them, and re-layouts, local(): element_basis = extended[:, :, corner_ids]  6.71 us
  transfers between devices with their start and end apart: 2, of which 0 were waited for; matrix products, arithmetic and copies ran while one was open for 4% of the time, Pallas kernels for 0%

commit v1 on v0

v1 whole, which is shorter than its diff:
```python
import jax
import jax.numpy as jnp
from jax import lax
from jax.experimental import pallas as pl
from jax.experimental.pallas import tpu as pltpu
from jax.sharding import Mesh
from jax.sharding import PartitionSpec as P

f32, bf16 = jnp.float32, jnp.bfloat16
VMEM = pl.BlockSpec(memory_space=pltpu.VMEM)
PITCH = 40
ELEMS = 65536.0


def iota(shape, dim):
    return lax.broadcasted_iota(jnp.int32, shape, dim)


def dot(a, b):
    return jnp.dot(a, b, preferred_element_type=f32)


def turned(x, by):
    by = by % 4
    return x if by == 0 else pltpu.roll(x, 32 * by, 1)


def pick(pieces, quarter):
    out = pieces[0]
    for q in range(1, 4):
        out = jnp.where(quarter == q, pieces[q], out)
    return out


def in_group(rolled, rows, group, quarter):
    return pick([rolled[(q - group) % 4][rows[q] : rows[q] + 1, :] for q in range(4)], quarter)


def corner_rows(conn, quarter):
    conns = [turned(conn, by) for by in range(4)]
    return [
        jnp.concatenate(
            [in_group(conns, range(4 * h, 4 * h + 4), group, quarter) for h in range(2)], axis=1
        )
        for group in range(4)
    ]


def lane_quarter():
    return iota((1, 128), 1) >> 5


def own_element(lanes):
    return (iota((32, lanes), 1) & 31) == iota((32, lanes), 0)


def local_body(conn_ref, basis_ref, part_ref):
    ids = corner_rows(conn_ref[...], lane_quarter())
    nodes = basis_ref.shape[2]
    for group in range(4):
        hot = (iota((nodes, 256), 0) == ids[group]).astype(f32).astype(bf16)
        for k in range(3):
            part_ref[group, :, k * 256 : (k + 1) * 256] = dot(basis_ref[k], hot).astype(bf16)


def expanded_product(g_ref, x_ref, r_ref, group, pair, diagonal):
    for j in range(24):
        row = jnp.concatenate(
            [x_ref[group, j, 2 * pair + h : 2 * pair + h + 1, :] for h in range(2)], axis=1
        )
        r_ref[j * 32 : (j + 1) * 32, :] = jnp.where(diagonal, row, 0.0).astype(bf16)
    return dot(g_ref[group], r_ref[...])


def stats_body(
    conn_ref, mod_ref, stiff_ref, coords_ref, part_ref, ghost_ref,
    g_ref, x_ref, sums_ref, w_ref, r_ref, d_ref,
):
    quarter = lane_quarter()
    wide, diagonal = own_element(768), own_element(256)
    stiff = stiff_ref[...]
    high = stiff.astype(bf16)
    low = (stiff - high.astype(f32)).astype(bf16)
    spread = ((iota((24, 768), 1) >> 5) == iota((24, 768), 0)).astype(f32).astype(bf16)
    for p, piece in enumerate((high, low)):
        rows = lax.dot_general(piece, spread, (((0,), (0,)), ((), ())), preferred_element_type=f32)
        for j in range(24):
            w_ref[p, j * 32 : (j + 1) * 32, :] = jnp.where(wide, rows[j : j + 1, :], 0.0).astype(bf16)
    ids = corner_rows(conn_ref[...], quarter)
    for group in range(4):
        hot = (iota((256, 256), 0) + 1024 == ids[group]).astype(f32).astype(bf16)
        for k in range(3):
            at = slice(k * 256, (k + 1) * 256)
            ghost = jnp.concatenate([ghost_ref[0, k], ghost_ref[1, k]], axis=1)
            g_ref[group, :, at] = part_ref[group, :, at] + dot(ghost, hot).astype(bf16)
    coords = coords_ref[...]
    for group in range(4):
        d_ref[group * 32 : (group + 1) * 32, :] = dot(coords, g_ref[group]).astype(bf16)
    disp = d_ref[...]
    linear = dot(disp, w_ref[0]) + dot(disp, w_ref[1])
    mods = [turned(mod_ref[...], by) for by in range(4)]
    sums = None
    for group in range(4):
        modulus = jnp.concatenate([in_group(mods, [0] * 4, group, quarter)] * 6, axis=1)
        at = slice(group * 32, (group + 1) * 32)
        d = disp[at, :].astype(f32)
        force = (modulus * (linear[at, :] + 0.25 * d * d * d)).astype(bf16)
        part = lax.dot_general(force, g_ref[group], (((1,), (1,)), ((), ())), preferred_element_type=f32)
        sums = part if sums is None else sums + part
        force = force.astype(f32)
        for c in range(6):
            rolls = [
                [turned(force[8 * t : 8 * t + 8, c * 128 : (c + 1) * 128], by) for by in range(4)]
                for t in range(4)
            ]
            for a in range(4):
                x_ref[group, c * 4 + a] = pick(
                    [rolls[(q - group) % 4][(q - a) % 4] for q in range(4)], quarter
                )
    norms = []
    for pair in range(4):
        total = None
        for group in range(4):
            columns = expanded_product(g_ref, x_ref, r_ref.at[group], group, pair, diagonal)
            norm = jnp.sqrt(jnp.sum(columns * columns, axis=0, keepdims=True))
            norm = jnp.concatenate(
                [turned(norm[:, h * 128 : (h + 1) * 128], -group) for h in range(2)], axis=0
            )
            total = norm if total is None else total + norm
        norms.append(total)
    norms = jnp.concatenate(norms, axis=0)
    norms = jnp.concatenate(
        [jnp.sum(jnp.where(quarter == t, norms, 0.0), axis=1, keepdims=True) for t in range(4)], axis=0
    )
    lane = iota((1, 128), 1)
    last = jnp.concatenate([sums[:, 256:], jnp.zeros((32, 384 - sums.shape[1]), f32)], axis=1)
    last = jnp.where((lane == 44) | (lane == 45), norms, last)
    for half in range(2):
        at = slice(16 * half, 16 * half + 16)
        sums_ref[half, 0:16, :] = sums[at, 0:128]
        sums_ref[half, 16:32, :] = sums[at, 128:256]
        sums_ref[half, 32:40, :] = last[at, :][0:8] + pltpu.roll(last[at, :][8:16], 64, 1)


def columns_body(g_ref, x_ref, columns_ref, r_ref, acc_ref):
    quarter, diagonal = lane_quarter(), own_element(256)
    modes = g_ref.shape[1]
    for pair in range(4):
        for group in range(4):
            acc_ref[group] = expanded_product(g_ref, x_ref, r_ref, group, pair, diagonal)
        for h in range(2):
            lanes = slice(h * 128, (h + 1) * 128)
            for t in range(4):
                out = turned(pick([acc_ref[(q - t) % 4, :, lanes] for q in range(4)], quarter), -t)
                columns_ref[pl.ds(8 * t + 2 * pair + h, modes, stride=PITCH), :] = out


def scaled_body(sums_ref, columns_ref, training_ref, target_ref):
    last = jnp.concatenate(
        [x for h in range(2) for x in (sums_ref[h, 32:40, :], pltpu.roll(sums_ref[h, 32:40, :], 64, 1))],
        axis=0,
    )
    scale = ELEMS / (last[:, 44:45] + last[:, 45:46])
    training_ref[...] = (columns_ref[...] * scale[None]).astype(bf16)

    @pl.when(pl.program_id(0) == 0)
    def _():
        wide = scale * (1.0 / 256.0)
        for h in range(2):
            at = slice(16 * h, 16 * h + 16)
            target_ref[at, 0:128] = sums_ref[h, 0:16, :] * wide[at]
            target_ref[at, 128:256] = sums_ref[h, 16:32, :] * wide[at]
        target_ref[:, 256:300] = (last * wide)[:, 0:44]


def kernel(body, out, ins, scratch=(), flops=0):
    size = sum(x.size * x.dtype.itemsize for x in (*ins, *out))
    return pl.pallas_call(
        body,
        out_shape=out,
        in_specs=[VMEM] * len(ins),
        out_specs=(VMEM,) * len(out),
        scratch_shapes=scratch,
        compiler_params=pltpu.CompilerParams(vmem_limit_bytes=40 * 2**20),
        cost_estimate=pl.CostEstimate(flops=flops, bytes_accessed=size, transcendentals=0),
    )(*ins)


def array(shape, dtype):
    return jax.ShapeDtypeStruct(shape, dtype)


def passed_along(value, axis, by):
    peers = lax.axis_size(axis)
    return lax.ppermute(value, axis, [(i, (i + by) % peers) for i in range(peers)])


def from_each(value, axis):
    peers = lax.axis_size(axis)
    copies = jnp.broadcast_to(value[None], (peers, *value.shape))
    return lax.all_to_all(copies, axis, 0, 0, tiled=True)


def local(coords, basis_rows, connectivity, modulus, stiffness):
    modes = basis_rows.shape[1]
    core = lax.axis_index("core")
    own_half = lax.dynamic_slice_in_dim(basis_rows, core * 128, 128, axis=2)
    ghost_half = passed_along(own_half, ("z", "x"), -1)
    all_coords = from_each(coords, ("y", "core")).reshape(-1, modes)
    corner_ids = connectivity.T
    (part,) = kernel(
        local_body, (array((4, modes, 768), bf16),), (corner_ids, basis_rows), flops=2 * 10**9
    )
    ghost = lax.all_gather(ghost_half, "core")
    rows, forces, sums = kernel(
        stats_body,
        (array((4, modes, 768), bf16), array((4, 24, 8, 128), f32), array((2, 40, 128), f32)),
        (corner_ids, modulus.reshape(1, -1), stiffness, all_coords, part, ghost),
        (pltpu.VMEM((2, 768, 768), bf16), pltpu.VMEM((4, 768, 256), bf16), pltpu.VMEM((128, 768), bf16)),
        flops=3 * 10**9,
    )
    (columns,) = kernel(
        columns_body,
        (array((modes * PITCH, 128), f32),),
        (rows, forces),
        (pltpu.VMEM((768, 256), bf16), pltpu.VMEM((4, modes, 256), f32)),
        flops=2 * 10**9,
    )
    both = lax.all_gather(sums, "core")
    half = lax.dynamic_index_in_dim(both[0] + both[1], core, 0, keepdims=False)
    half = from_each(half, ("x", "y")).sum(axis=0)
    place = lax.broadcasted_iota(jnp.int32, half.shape, 0) >= 32
    lane = lax.broadcasted_iota(jnp.int32, half.shape, 1) & 63
    rounded = lax.reduce_precision(half, 8, 7)
    half = jnp.where(place & (lane == 45), half - rounded, half).astype(bf16)
    half = from_each(half, "z").astype(f32).sum(axis=0)
    totals = lax.all_gather(half, "core")
    step = 60
    training, target = pl.pallas_call(
        scaled_body,
        grid=(modes // step,),
        out_shape=(array((modes, 32, 128), bf16), array((32, modes), f32)),
        in_specs=[
            pl.BlockSpec((2, 40, 128), lambda i: (0, 0, 0)),
            pl.BlockSpec((step, 32, 128), lambda i: (i, 0, 0)),
        ],
        out_specs=(
            pl.BlockSpec((step, 32, 128), lambda i: (i, 0, 0)),
            pl.BlockSpec((32, modes), lambda i: (0, 0)),
        ),
        compiler_params=pltpu.CompilerParams(vmem_limit_bytes=20 * 2**20),
    )(totals, columns.reshape(modes, PITCH, 128))
    return training.transpose(1, 0, 2), target


def solution(mesh):
    split = Mesh(mesh.devices.reshape(16, 4, 4, 2), ("z", "x", "y", "core"))
    elem, param = ("z", "x"), ("y", "core")
    return jax.shard_map(
        local,
        mesh=split,
        in_specs=(P(param, None), P(None, None, elem), P(elem + param, None), P(elem + param), P()),
        out_specs=(P(None, None, elem + param), P()),
        check_vma=False,
    )
```

time: 169 us -> 83.6 us (0.49)
  blocking collectives: 59.4 us -> 10.4 us
  other arithmetic: 37.9 us -> 0.15 us
  local copies, waits for them, and re-layouts: 39.9 us -> 14 us
  waiting for transfers between devices: 0.01 us -> 14.8 us
  Pallas kernels: 0 us -> 12.9 us
  matrix products: 10.8 us -> 0 us
  starting transfers between devices: 19.6 us -> 30.1 us
    all_to_all x4 -> x0, blocking collectives: 59.4 us -> none  [the longest x2 27.8 us: copy_for_each(): lax.all_to_all(jnp.broadcast_to(value[None], (peers, *value.shape)), axis...]
    concatenate x3 -> x0, other arithmetic: 31.2 us -> none  [the longest x2 31.1 us: local(): extended = jnp.concatenate([basis_rows, ghost_rows], axis=2)]
    all_to_all x1 -> x3, waiting for transfers between devices: 0.01 us -> 14.8 us  [from_each(): return lax.all_to_all(copies, axis, 0, 0, tiled=True)]
    pallas_call x0 -> x4, Pallas kernels: none -> 12.9 us  [the longest x3 9.36 us: kernel(): pl.pallas_call(body, out_shape=out, in_specs=[VMEM] * len(ins), out_specs...]
    slice x5 -> x1, local copies, waits for them, and re-layouts: 12.5 us -> 0.01 us  [local(): half = lax.dynamic_index_in_dim(both[0] + both[1], core, 0, keepdims=False)]
    gather x3 -> x0, local copies, waits for them, and re-layouts: 10.8 us -> none  [the longest x1 6.71 us: local(): element_basis = extended[:, :, corner_ids]]
    dot_general x5 -> x0, matrix products: 10.8 us -> none  [the longest x1 6.23 us: local(): jnp.einsum('cmae,scae->sme', element_basis, forces, preferred_element_typ...]
    all_to_all x1 -> x3, starting transfers between devices: 5.42 us -> 15.9 us  [from_each(): return lax.all_to_all(copies, axis, 0, 0, tiled=True)]
  transfers between devices with their start and end apart: 2 -> 4, of which waited for: 0 -> 2; matrix products, arithmetic and copies ran while one was open for 4% -> 2% of each run, Pallas kernels for 0% -> 6%
where the time goes in v1:
time: 83.6 us; the launch traced here: 83.1 us
  starting transfers between devices  30.1 us (36%)
  waiting for transfers between devices  14.8 us (18%)
  local copies, waits for them, and re-layouts  14 us (17%)
  Pallas kernels  12.9 us (15%)
  blocking collectives  10.4 us (12%)
    all_to_all x3, starting transfers between devices, from_each(): return lax.all_to_all(copies, axis, 0, 0, tiled=True)  15.9 us
    all_to_all x3, waiting for transfers between devices, from_each(): return lax.all_to_all(copies, axis, 0, 0, tiled=True)  14.8 us
    ppermute x1, starting transfers between devices, passed_along(): lax.ppermute(value, axis, [(i, (i + by) % peers) for i in range(peers)])  14.1 us
    unnamed x18, local copies, waits for them, and re-layouts  10.3 us
    pallas_call x3, Pallas kernels, kernel(): pl.pallas_call(body, out_shape=out, in_specs=[VMEM] * len(ins), out_specs...  9.36 us
    all_gather x1, blocking collectives, local(): totals = lax.all_gather(half, 'core')  6.39 us
    pallas_call x1, Pallas kernels, local(): pl.pallas_call(scaled_body, grid=(modes // step,), out_shape=(array((mode...  3.51 us
    broadcast_in_dim x3, local copies, waits for them, and re-layouts, from_each(): copies = jnp.broadcast_to(value[None], (peers, *value.shape))  2.74 us
  transfers between devices with their start and end apart: 4, of which 2 were waited for; matrix products, arithmetic and copies ran while one was open for 2% of the time, Pallas kernels for 6%

profile of v1, /device:TPU:1, one launch (start us, length us, event | category | flops | bytes accessed | tf_op | source)
XLA Modules:
  0.0 83.1 jit_solution(17015474942684758715)
XLA Ops:
  0.6 1.0 %constant_dynamic-slice_fusion = bf16[3,300,128]{2,1,0:T(8,128)(2,1)S(1)} fusion(bf16[3,300,1024]{2,1,0:T(8,128)(2,1)} %basis_ref.1, s32[]{:T(128)S(6)} %select_n.15), kind=kLoop, calls=%fused_computation.5 | loop fusion | bytes 460804 | tf_op jit(solution)/shard_map/dynamic_slice | solution.py:207
  1.6 14.1 %collective-permute-start = (bf16[3,300,128]{2,1,0:T(8,128)(2,1)S(1)}, bf16[3,300,128]{2,1,0:T(8,128)(2,1)S(1)}, u32[]{:S(2)}, u32[]{:S(2)}) collective-permute-start(bf16[3,300,128]{2,1,0:T(8,128)(2,1)S(1)} %constant_dynamic-slice_fusion), channel_id=1, source_target_pairs={{0,504},{8,0},{16,8},{24,16},{32,24},{40,32},{48,40},{56,48},{64,5... | collective-permute-start | bytes 691208 | tf_op jit(solution)/shard_map/ppermute | solution.py:195
  15.8 1.3 %broadcast_in_dim.8 = bf16[8,4,300]{2,1,0:T(4,128)(2,1)} broadcast(bf16[4,300]{1,0:T(4,128)(2,1)} %param.5), dimensions={1,2} | broadcast | bytes 21600 | tf_op jit(solution)/shard_map/broadcast_in_dim | solution.py:200
  17.1 5.4 %all-to-all-start = ((bf16[8,4,300]{2,1,0:T(4,128)(2,1)}), bf16[8,4,300]{2,1,0:T(4,128)(2,1)S(1)}, u32[]{:S(2)}, u32[]{:S(2)}) async-start(bf16[8,4,300]{2,1,0:T(4,128)(2,1)} %broadcast_in_dim.8), calls=%async_computation | async-start | bytes 49152 | tf_op jit(solution)/shard_map/all_to_all | solution.py:201
  22.5 0.0 copy-start.2
  22.5 1.5 %copy-done.2 = bf16[3,300,1024]{2,1,0:T(8,128)(2,1)S(1)} copy-done((bf16[3,300,1024]{2,1,0:T(8,128)(2,1)S(1)}, bf16[3,300,1024]{2,1,0:T(8,128)(2,1)}, u32[]{:S(2)}) %copy-start.2) | copy-done | bytes 1843224
  24.0 0.0 copy-start.4
  24.0 0.7 copy-done.4
  24.7 0.0 copy-start.3
  24.7 0.0 copy-start.5
  24.7 0.0 copy-start.6
  24.7 2.2 %shard_map.68.part_ref = bf16[4,300,768]{2,1,0:T(8,128)(2,1)S(1)} custom-call(s32[8,128]{1,0:T(8,128)S(1)} %bitcast.11, bf16[3,300,1024]{2,1,0:T(8,128)(2,1)S(1)} %copy-done.2), custom_call_target="tpu_custom_call" | custom-call | flops 2000000000 | bytes 3690496 | tf_op jit(solution)/shard_map/pallas_call | solution.py:178
  26.9 0.0 copy-start.7
  26.9 1.2 %copy-done.7 = bf16[4,300,768]{2,1,0:T(8,128)(2,1)} copy-done((bf16[4,300,768]{2,1,0:T(8,128)(2,1)}, bf16[4,300,768]{2,1,0:T(8,128)(2,1)S(1)}, u32[]{:S(2)}) %copy-start.7) | copy-done | bytes 1843224
  28.1 0.0 all-to-all-done
  28.1 0.0 collective-permute-done
  28.2 2.1 %all-gather = bf16[6,300,128]{2,1,0:T(8,128)(2,1)S(1)} all-gather(bf16[3,300,128]{2,1,0:T(8,128)(2,1)S(1)} %collective-permute-done), channel_id=2, replica_groups=mesh['z'=16,'x'=4,'y'=4,'core'=2] {'core'}, dimensions={0}, use_global_device_ids=true | all-gather | bytes 691200 | tf_op jit(solution)/shard_map/all_gather | solution.py:214
  30.3 0.0 copy-done.3
  30.3 0.0 copy-done.5
  30.3 0.0 copy-done.6
  30.3 0.0 copy-start.8
  30.3 1.5 %copy-done.8 = bf16[4,300,768]{2,1,0:T(8,128)(2,1)S(1)} copy-done((bf16[4,300,768]{2,1,0:T(8,128)(2,1)S(1)}, bf16[4,300,768]{2,1,0:T(8,128)(2,1)}, u32[]{:S(2)}) %copy-start.8) | copy-done | bytes 1843224
  31.8 4.4 %shard_map.69 = (bf16[4,300,768]{2,1,0:T(8,128)(2,1)S(1)}, f32[4,24,8,128]{3,2,1,0:T(8,128)S(1)}, f32[2,40,128]{2,1,0:T(8,128)S(1)}) custom-call(s32[8,128]{1,0:T(8,128)S(1)} %bitcast.12, f32[1,128]{1,0:T(1,128)S(1)} %bitcast.13, f32[24,24]{1,0:T(8,128)S(1)} %copy-done.3, bf16[32,300]{1,0:T(8,128)(2,1)S(1)} %reshape.47.coords_ref, ...), custom_call_target="tpu_custom_call" | custom-call | flops 3000000000 | bytes 4607488 | tf_op jit(solution)/shard_map/pallas_call | solution.py:178
  36.3 1.9 %all-gather.1 = f32[4,40,128]{2,1,0:T(8,128)S(1)} all-gather(f32[2,40,128]{2,1,0:T(8,128)S(1)} %get-tuple-element.7), channel_id=3, replica_groups=mesh['z'=16,'x'=4,'y'=4,'core'=2] {'core'}, dimensions={0}, use_global_device_ids=true | all-gather | bytes 122880 | tf_op jit(solution)/shard_map/all_gather | solution.py:229
  38.2 0.7 broadcast_in_dim.10
  38.9 4.3 %all-to-all-start.1 = ((f32[16,40,128]{2,1,0:T(8,128)}), f32[16,40,128]{2,1,0:T(8,128)S(1)}, u32[]{:S(2)}, u32[]{:S(2)}) async-start(f32[16,40,128]{2,1,0:T(8,128)} %broadcast_in_dim.10), calls=%async_computation.1 | async-start | bytes 655360 | tf_op jit(solution)/shard_map/all_to_all | solution.py:201
  43.2 7.9 %all-to-all-done.1 = f32[16,40,128]{2,1,0:T(8,128)S(1)} async-done(((f32[16,40,128]{2,1,0:T(8,128)}), f32[16,40,128]{2,1,0:T(8,128)S(1)}, u32[]{:S(2)}, u32[]{:S(2)}) %all-to-all-start.1) | async-done | bytes 327712 | tf_op jit(solution)/shard_map/all_to_all | solution.py:201
  51.2 0.1 fusion
  51.2 0.7 broadcast_in_dim.11
  51.9 6.3 %all-to-all-start.2 = ((bf16[16,40,128]{2,1,0:T(8,128)(2,1)}), bf16[16,40,128]{2,1,0:T(8,128)(2,1)S(1)}, u32[]{:S(2)}, u32[]{:S(2)}) async-start(bf16[16,40,128]{2,1,0:T(8,128)(2,1)} %broadcast_in_dim.11), calls=%async_computation.2 | async-start | bytes 327680 | tf_op jit(solution)/shard_map/all_to_all | solution.py:201
  58.2 2.7 %shard_map.70 = f32[12000,128]{1,0:T(8,128)S(1)} custom-call(bf16[4,300,768]{2,1,0:T(8,128)(2,1)S(1)} %get-tuple-element.8.g_ref, f32[4,24,8,128]{3,2,1,0:T(8,128)S(1)} %get-tuple-element.9.x_ref), custom_call_target="tpu_custom_call" | custom-call | flops 2000000000 | bytes 8380416 | tf_op jit(solution)/shard_map/pallas_call | solution.py:178
  60.9 0.0 copy-start
  60.9 2.6 %copy-done = f32[12000,128]{1,0:T(8,128)} copy-done((f32[12000,128]{1,0:T(8,128)}, f32[12000,128]{1,0:T(8,128)S(1)}, u32[]{:S(2)}) %copy-start) | copy-done | bytes 6144024
  63.5 6.9 %all-to-all-done.2 = bf16[16,40,128]{2,1,0:T(8,128)(2,1)S(1)} async-done(((bf16[16,40,128]{2,1,0:T(8,128)(2,1)}), bf16[16,40,128]{2,1,0:T(8,128)(2,1)S(1)}, u32[]{:S(2)}, u32[]{:S(2)}) %all-to-all-start.2) | async-done | bytes 163872 | tf_op jit(solution)/shard_map/all_to_all | solution.py:201
  70.4 6.4 %all-gather.2 = f32[80,128]{1,0:T(8,128)S(1)} all-gather(f32[40,128]{1,0:T(8,128)S(1)} %convert_reduce_fusion), channel_id=4, replica_groups=mesh['z'=16,'x'=4,'y'=4,'core'=2] {'core'}, dimensions={0}, use_global_device_ids=true | all-gather | bytes 61440 | tf_op jit(solution)/shard_map/all_gather | solution.py:237
  76.8 0.0 copy-start.1
  76.8 2.7 %copy-done.1 = f32[12000,128]{1,0:T(8,128)S(1)} copy-done((f32[12000,128]{1,0:T(8,128)S(1)}, f32[12000,128]{1,0:T(8,128)}, u32[]{:S(2)}) %copy-start.1) | copy-done | bytes 6144024
  79.6 3.5 %shard_map.71 = (bf16[300,32,128]{2,1,0:T(8,128)(2,1)}, f32[32,300]{1,0:T(8,128)}) custom-call(f32[2,40,128]{2,1,0:T(8,128)S(1)} %bitcast.10, f32[300,40,128]{2,1,0:T(8,128)S(1)} %bitcast.8), custom_call_target="tpu_custom_call" | custom-call | tf_op jit(solution)/shard_map/pallas_call | solution.py:239
  (7 shorter events, 0.1 us)
Async XLA Ops:
  1.6 26.6 %collective-permute-start = (bf16[3,300,128]{2,1,0:T(8,128)(2,1)S(1)}, bf16[3,300,128]{2,1,0:T(8,128)(2,1)S(1)}, u32[]{:S(2)}, u32[]{:S(2)}) collective-permute-start(bf16[3,300,128]{2,1,0:T(8,128)(2,1)S(1)} %constant_dynamic-slice_fusion), channel_id=1, source_target_pairs={{0,504},{8,0},{16,8},{24,16},{32,24},{40,32},{48,40},{56,48},{64,5... | collective-permute-start | bytes 691208 | tf_op jit(solution)/shard_map/ppermute | solution.py:195
  17.1 11.1 %all-to-all-start = ((bf16[8,4,300]{2,1,0:T(4,128)(2,1)}), bf16[8,4,300]{2,1,0:T(4,128)(2,1)S(1)}, u32[]{:S(2)}, u32[]{:S(2)}) async-start(bf16[8,4,300]{2,1,0:T(4,128)(2,1)} %broadcast_in_dim.8), calls=%async_computation | async-start | bytes 49152 | tf_op jit(solution)/shard_map/all_to_all | solution.py:201
  22.5 1.5 %copy-start.2 = (bf16[3,300,1024]{2,1,0:T(8,128)(2,1)S(1)}, bf16[3,300,1024]{2,1,0:T(8,128)(2,1)}, u32[]{:S(2)}) copy-start(bf16[3,300,1024]{2,1,0:T(8,128)(2,1)} %basis_ref.1) | copy-start | bytes 5529604
  24.0 0.7 copy-start.4
  24.7 5.6 %copy-start.3 = (f32[24,24]{1,0:T(8,128)S(1)}, f32[24,24]{1,0:T(8,128)}, u32[]{:S(2)}) copy-start(f32[24,24]{1,0:T(8,128)} %stiff_ref.1) | copy-start | bytes 6916
  24.7 5.6 %copy-start.5 = (s32[128,8]{0,1:T(8,128)S(1)}, s32[128,8]{0,1:T(8,128)}, u32[]{:S(2)}) copy-start(s32[128,8]{0,1:T(8,128)} %param.7) | copy-start | bytes 12292
  24.7 5.6 %copy-start.6 = (f32[128]{0:T(128)S(1)}, f32[128]{0:T(128)}, u32[]{:S(2)}) copy-start(f32[128]{0:T(128)} %param.8) | copy-start | bytes 1540
  26.9 1.2 %copy-start.7 = (bf16[4,300,768]{2,1,0:T(8,128)(2,1)}, bf16[4,300,768]{2,1,0:T(8,128)(2,1)S(1)}, u32[]{:S(2)}) copy-start(bf16[4,300,768]{2,1,0:T(8,128)(2,1)S(1)} %shard_map.68.part_ref) | copy-start | bytes 5529604
  30.3 1.5 %copy-start.8 = (bf16[4,300,768]{2,1,0:T(8,128)(2,1)S(1)}, bf16[4,300,768]{2,1,0:T(8,128)(2,1)}, u32[]{:S(2)}) copy-start(bf16[4,300,768]{2,1,0:T(8,128)(2,1)} %copy-done.7) | copy-start | bytes 5529604
  38.9 12.2 %all-to-all-start.1 = ((f32[16,40,128]{2,1,0:T(8,128)}), f32[16,40,128]{2,1,0:T(8,128)S(1)}, u32[]{:S(2)}, u32[]{:S(2)}) async-start(f32[16,40,128]{2,1,0:T(8,128)} %broadcast_in_dim.10), calls=%async_computation.1 | async-start | bytes 655360 | tf_op jit(solution)/shard_map/all_to_all | solution.py:201
  51.9 18.5 %all-to-all-start.2 = ((bf16[16,40,128]{2,1,0:T(8,128)(2,1)}), bf16[16,40,128]{2,1,0:T(8,128)(2,1)S(1)}, u32[]{:S(2)}, u32[]{:S(2)}) async-start(bf16[16,40,128]{2,1,0:T(8,128)(2,1)} %broadcast_in_dim.11), calls=%async_computation.2 | async-start | bytes 327680 | tf_op jit(solution)/shard_map/all_to_all | solution.py:201
  60.9 2.6 %copy-start = (f32[12000,128]{1,0:T(8,128)}, f32[12000,128]{1,0:T(8,128)S(1)}, u32[]{:S(2)}) copy-start(f32[12000,128]{1,0:T(8,128)S(1)} %shard_map.70) | copy-start | bytes 18432004
  76.8 2.7 %copy-start.1 = (f32[12000,128]{1,0:T(8,128)S(1)}, f32[12000,128]{1,0:T(8,128)}, u32[]{:S(2)}) copy-start(f32[12000,128]{1,0:T(8,128)} %copy-done) | copy-start | bytes 18432004

commit v2 on v1

v2 whole, which is shorter than its diff:
```python
import jax
import jax.numpy as jnp
from jax import lax
from jax.experimental import pallas as pl
from jax.experimental.pallas import tpu as pltpu
from jax.sharding import Mesh
from jax.sharding import PartitionSpec as P

f32, bf16 = jnp.float32, jnp.bfloat16
VMEM = pl.BlockSpec(memory_space=pltpu.VMEM)
ANY = pl.BlockSpec(memory_space=pl.ANY)
DMA = pltpu.SemaphoreType.DMA
PITCH = 40
ELEMS = 65536.0


def iota(shape, dim):
    return lax.broadcasted_iota(jnp.int32, shape, dim)


def dot(a, b):
    return jnp.dot(a, b, preferred_element_type=f32)


def turned(x, by):
    by = by % 4
    return x if by == 0 else pltpu.roll(x, 32 * by, 1)


def pick(pieces, quarter):
    out = pieces[0]
    for q in range(1, 4):
        out = jnp.where(quarter == q, pieces[q], out)
    return out


def in_group(rolled, rows, group, quarter):
    return pick([rolled[(q - group) % 4][rows[q] : rows[q] + 1, :] for q in range(4)], quarter)


def corner_rows(conn, quarter):
    conns = [turned(conn, by) for by in range(4)]
    return [
        jnp.concatenate(
            [in_group(conns, range(4 * h, 4 * h + 4), group, quarter) for h in range(2)], axis=1
        )
        for group in range(4)
    ]


def lane_quarter():
    return iota((1, 128), 1) >> 5


def own_element(lanes):
    return (iota((32, lanes), 1) & 31) == iota((32, lanes), 0)


def prepare_body(core_ref, coords_ref, basis_ref, half_ref, copies_ref, sem):
    at = pl.ds(pl.multiple_of(core_ref[0] * 128, 128), 128)
    loads = [pltpu.make_async_copy(basis_ref.at[k, :, at], half_ref.at[k], sem.at[k]) for k in range(3)]
    loads += [pltpu.make_async_copy(coords_ref, copies_ref.at[i], sem.at[3 + i]) for i in range(8)]
    for load in loads:
        load.start()
    for load in loads:
        load.wait()


def expanded_product(g_ref, x_ref, r_ref, group, pair, diagonal):
    for j in range(24):
        row = jnp.concatenate(
            [x_ref[group, j, 2 * pair + h : 2 * pair + h + 1, :] for h in range(2)], axis=1
        )
        r_ref[j * 32 : (j + 1) * 32, :] = jnp.where(diagonal, row, 0.0).astype(bf16)
    return dot(g_ref[group], r_ref[...])


def stats_body(
    conn_ref, mod_ref, stiff_ref, coords_ref, basis_ref, ghost_ref,
    columns_ref, sums_ref, g_ref, x_ref, w_ref, r_ref, d_ref, acc_ref, wide_ref,
):
    quarter = lane_quarter()
    wide, diagonal = own_element(768), own_element(256)
    stiff = stiff_ref[...]
    high = stiff.astype(bf16)
    low = (stiff - high.astype(f32)).astype(bf16)
    spread = ((iota((24, 768), 1) >> 5) == iota((24, 768), 0)).astype(f32).astype(bf16)
    for p, piece in enumerate((high, low)):
        rows = lax.dot_general(piece, spread, (((0,), (0,)), ((), ())), preferred_element_type=f32)
        for j in range(24):
            w_ref[p, j * 32 : (j + 1) * 32, :] = jnp.where(wide, rows[j : j + 1, :], 0.0).astype(bf16)
    ids = corner_rows(conn_ref[...], quarter)
    modes, nodes = basis_ref.shape[1:]
    for group in range(4):
        hot = (iota((nodes, 256), 0) == ids[group]).astype(f32).astype(bf16)
        hot_ghost = (iota((256, 256), 0) + nodes == ids[group]).astype(f32).astype(bf16)
        for k in range(3):
            ghost = jnp.concatenate([ghost_ref[0, k], ghost_ref[1, k]], axis=1)
            rows = dot(basis_ref[k], hot) + dot(ghost, hot_ghost)
            g_ref[group, :, k * 256 : (k + 1) * 256] = rows.astype(bf16)
    coords = coords_ref[...]
    for group in range(4):
        d_ref[group * 32 : (group + 1) * 32, :] = dot(coords, g_ref[group]).astype(bf16)
    disp = d_ref[...]
    linear = dot(disp, w_ref[0]) + dot(disp, w_ref[1])
    mods = [turned(mod_ref[...], by) for by in range(4)]
    sums = None
    for group in range(4):
        modulus = jnp.concatenate([in_group(mods, [0] * 4, group, quarter)] * 6, axis=1)
        at = slice(group * 32, (group + 1) * 32)
        d = disp[at, :].astype(f32)
        force = (modulus * (linear[at, :] + 0.25 * d * d * d)).astype(bf16)
        part = lax.dot_general(force, g_ref[group], (((1,), (1,)), ((), ())), preferred_element_type=f32)
        sums = part if sums is None else sums + part
        force = force.astype(f32)
        for c in range(6):
            rolls = [
                [turned(force[8 * t : 8 * t + 8, c * 128 : (c + 1) * 128], by) for by in range(4)]
                for t in range(4)
            ]
            for a in range(4):
                x_ref[group, c * 4 + a] = pick(
                    [rolls[(q - group) % 4][(q - a) % 4] for q in range(4)], quarter
                )
    norms = []
    for pair in range(4):
        total = None
        for group in range(4):
            columns = expanded_product(g_ref, x_ref, r_ref.at[group], group, pair, diagonal)
            acc_ref[group] = columns
            norm = jnp.sqrt(jnp.sum(columns * columns, axis=0, keepdims=True))
            norm = jnp.concatenate(
                [turned(norm[:, h * 128 : (h + 1) * 128], -group) for h in range(2)], axis=0
            )
            total = norm if total is None else total + norm
        norms.append(total)
        for h in range(2):
            lanes = slice(h * 128, (h + 1) * 128)
            for t in range(4):
                out = turned(pick([acc_ref[(q - t) % 4, :, lanes] for q in range(4)], quarter), -t)
                wide_ref[pl.ds(8 * t + 2 * pair + h, modes, stride=PITCH), :] = out
    norms = jnp.concatenate(norms, axis=0)
    norms = jnp.concatenate(
        [jnp.sum(jnp.where(quarter == t, norms, 0.0), axis=1, keepdims=True) for t in range(4)], axis=0
    )
    lane = iota((1, 128), 1)
    last = jnp.concatenate([sums[:, 256:], jnp.zeros((32, 384 - sums.shape[1]), f32)], axis=1)
    rounded = norms.astype(bf16).astype(f32)
    last = jnp.where(lane == 44, rounded, jnp.where(lane == 45, norms - rounded, last))
    for half in range(2):
        at = slice(16 * half, 16 * half + 16)
        packed = jnp.concatenate(
            [
                sums[at, 0:128],
                sums[at, 128:256],
                last[at, :][0:8] + pltpu.roll(last[at, :][8:16], 64, 1),
            ],
            axis=0,
        ).astype(bf16)
        for peer in range(16):
            sums_ref[peer, half] = packed

    def narrow(i, _):
        for j in range(10):
            at = pl.multiple_of((i * 10 + j) * PITCH, 8)
            columns_ref[i * 10 + j] = wide_ref[pl.ds(at, 32), :].astype(bf16)

    lax.fori_loop(0, modes // 10, narrow, None)


def middle_body(arrived_ref, out_ref):
    total = jnp.sum(arrived_ref[...].astype(f32), axis=0)
    row, lane = iota((40, 128), 0), iota((40, 128), 1) & 63
    whole = total + pltpu.roll(total, 127, 1)
    rounded = whole.astype(bf16).astype(f32)
    total = jnp.where((row >= 32) & (lane == 44), rounded, total)
    total = jnp.where((row >= 32) & (lane == 45), pltpu.roll(whole - rounded, 1, 1), total)
    out_ref[...] = jnp.broadcast_to(total.astype(bf16)[None], out_ref.shape)


def scaled_body(sums_ref, columns_ref, training_ref, target_ref, out_ref, sem):
    last = jnp.concatenate(
        [x for h in range(2) for x in (sums_ref[h, 32:40, :], pltpu.roll(sums_ref[h, 32:40, :], 64, 1))],
        axis=0,
    )
    scale = ELEMS / (last[:, 44:45] + last[:, 45:46])
    wide = jnp.broadcast_to(scale, (32, 128))
    steps, step = out_ref.shape[0], out_ref.shape[1]
    stores = []
    for i in range(steps):
        at = slice(i * step, (i + 1) * step)
        out_ref[i] = (columns_ref[at].astype(f32) * wide[None]).astype(bf16)
        stores.append(pltpu.make_async_copy(out_ref.at[i], training_ref.at[at], sem.at[i]))
        stores[-1].start()
    scale = scale * (1.0 / 256.0)
    for h in range(2):
        at = slice(16 * h, 16 * h + 16)
        target_ref[at, 0:128] = sums_ref[h, 0:16, :] * scale[at]
        target_ref[at, 128:256] = sums_ref[h, 16:32, :] * scale[at]
    target_ref[:, 256:300] = (last * scale)[:, 0:44]
    for store in stores:
        store.wait()


def kernel(body, out, ins, scratch=(), flops=0, far=(), scalars=0, room=16):
    size = sum(x.size * x.dtype.itemsize for x in (*ins, *out))
    specs = [ANY if i in far else VMEM for i in range(len(ins) + len(out))]
    specs[:scalars] = [pl.BlockSpec(memory_space=pltpu.SMEM)] * scalars
    return pl.pallas_call(
        body,
        out_shape=out,
        in_specs=specs[: len(ins)],
        out_specs=tuple(specs[len(ins) :]),
        scratch_shapes=scratch,
        compiler_params=pltpu.CompilerParams(vmem_limit_bytes=room * 2**20),
        cost_estimate=pl.CostEstimate(flops=flops, bytes_accessed=size, transcendentals=0),
    )(*ins)


def array(shape, dtype):
    return jax.ShapeDtypeStruct(shape, dtype)


def passed_along(value, axis, by):
    peers = lax.axis_size(axis)
    return lax.ppermute(value, axis, [(i, (i + by) % peers) for i in range(peers)])


def exchanged(copies, axis):
    return lax.all_to_all(copies, axis, 0, 0, tiled=True)


def local(coords, basis_rows, connectivity, modulus, stiffness):
    modes = basis_rows.shape[1]
    core = lax.axis_index("core")
    own_half, copies = kernel(
        prepare_body,
        (array((3, modes, 128), bf16), array((8, *coords.shape), bf16)),
        (core.astype(jnp.int32).reshape(1), coords, basis_rows),
        (DMA((11,)),),
        far=(1, 2),
        scalars=1,
        room=59,
    )
    ghost_half = passed_along(own_half, ("z", "x"), -1)
    all_coords = exchanged(copies, ("y", "core")).reshape(-1, modes)
    ghost = lax.all_gather(ghost_half, "core")
    rows_shape = (4, modes, 768)
    columns, sums = kernel(
        stats_body,
        (array((modes, 32, 128), bf16), array((16, 2, 40, 128), bf16)),
        (connectivity.T, modulus.reshape(1, -1), stiffness, all_coords, basis_rows, ghost),
        (
            pltpu.VMEM((4, modes, 768), bf16),
            pltpu.VMEM((4, 24, 8, 128), f32),
            pltpu.VMEM((2, 768, 768), bf16),
            pltpu.VMEM((4, 768, 256), bf16),
            pltpu.VMEM((128, 768), bf16),
            pltpu.VMEM((4, modes, 256), f32),
            pltpu.VMEM((modes * PITCH, 128), f32),
        ),
        flops=7 * 10**9,
        room=24,
    )
    plane = exchanged(sums.reshape(32, 40, 128), ("x", "y", "core"))
    (plane,) = kernel(middle_body, (array((16, 40, 128), bf16),), (plane,))
    half = exchanged(plane, "z").astype(f32).sum(axis=0)
    totals = lax.all_gather(half, "core")
    step = 60
    training, target = kernel(
        scaled_body,
        (array((modes, 32, 128), bf16), array((32, modes), f32)),
        (totals, columns),
        (pltpu.VMEM((modes // step, step, 32, 128), bf16), DMA((modes // step,))),
        far=(2,),
    )
    return training.transpose(1, 0, 2), target


def solution(mesh):
    split = Mesh(mesh.devices.reshape(16, 4, 4, 2), ("z", "x", "y", "core"))
    elem, param = ("z", "x"), ("y", "core")
    return jax.shard_map(
        local,
        mesh=split,
        in_specs=(P(param, None), P(None, None, elem), P(elem + param, None), P(elem + param), P()),
        out_specs=(P(None, None, elem + param), P()),
        check_vma=False,
    )
```

time: 83.6 us -> 75.7 us (0.906)
  blocking collectives: 10.4 us -> 48.5 us
  starting transfers between devices: 30.1 us -> 14.1 us
  waiting for transfers between devices: 14.8 us -> 0.01 us
  local copies, waits for them, and re-layouts: 14 us -> 0.04 us
  Pallas kernels: 12.9 us -> 11.9 us
    all_to_all x0 -> x3, blocking collectives: none -> 42.5 us  [exchanged(): return lax.all_to_all(copies, axis, 0, 0, tiled=True)]
    all_to_all x3 -> x0, starting transfers between devices: 15.9 us -> none  [from_each(): return lax.all_to_all(copies, axis, 0, 0, tiled=True)]
    all_to_all x3 -> x0, waiting for transfers between devices: 14.8 us -> none  [from_each(): return lax.all_to_all(copies, axis, 0, 0, tiled=True)]
    unnamed x18 -> x8, local copies, waits for them, and re-layouts: 10.3 us -> 0.02 us
    all_gather x1, blocking collectives: 6.39 us -> 3.58 us  [local(): totals = lax.all_gather(half, 'core')]
    broadcast_in_dim x3 -> x0, local copies, waits for them, and re-layouts: 2.74 us -> none  [from_each(): copies = jnp.broadcast_to(value[None], (peers, *value.shape))]
    all_gather x1 -> x0, blocking collectives: 1.86 us -> none  [local(): both = lax.all_gather(sums, 'core')]
    dynamic_slice x1 -> x0, local copies, waits for them, and re-layouts: 0.96 us -> none  [local(): own_half = lax.dynamic_slice_in_dim(basis_rows, core * 128, 128, axis=2)]
  transfers between devices with their start and end apart: 4 -> 1, of which waited for: 2 -> 0; matrix products, arithmetic and copies ran while one was open for 2% -> 0% of each run, Pallas kernels for 6% -> 0%
where the time goes in v2:
time: 75.7 us; the launch traced here: 75.4 us
  blocking collectives  48.5 us (64%)
  starting transfers between devices  14.1 us (19%)
  Pallas kernels  11.9 us (16%)
    all_to_all x3, blocking collectives, exchanged(): return lax.all_to_all(copies, axis, 0, 0, tiled=True)  42.5 us
    ppermute x1, starting transfers between devices, passed_along(): lax.ppermute(value, axis, [(i, (i + by) % peers) for i in range(peers)])  14.1 us
    pallas_call x4, Pallas kernels, kernel(): pl.pallas_call(body, out_shape=out, in_specs=specs[:len(ins)], out_specs=...  11.9 us
    all_gather x1, blocking collectives, local(): totals = lax.all_gather(half, 'core')  3.58 us
    all_gather x1, blocking collectives, local(): ghost = lax.all_gather(ghost_half, 'core')  2.49 us
  transfers between devices with their start and end apart: 1, of which 0 were waited for; matrix products, arithmetic and copies ran while one was open for 0% of the time, Pallas kernels for 0%

profile of v2, /device:TPU:1, one launch (start us, length us, event | category | flops | bytes accessed | tf_op | source)
XLA Modules:
  0.0 75.4 jit_solution(14110349640530868974)
XLA Ops:
  0.6 0.0 copy-start
  0.6 0.0 copy-start.1
  0.7 0.0 copy-start.3
  0.7 0.0 copy-start.2
  0.7 1.9 %shard_map.68 = (bf16[3,300,128]{2,1,0:T(8,128)(2,1)}, bf16[8,4,300]{2,1,0:T(4,128)(2,1)}) custom-call(s32[1]{0:T(128)} %bitcast.2.core_ref, bf16[4,300]{1,0:T(4,128)(2,1)} %coords_ref.1, bf16[3,300,1024]{2,1,0:T(8,128)(2,1)} %basis_ref.3), custom_call_target="tpu_custom_call" | custom-call | bytes 2095204 | tf_op jit(solution)/shard_map/pallas_call | solution.py:209
  2.6 14.1 %collective-permute-start = (bf16[3,300,128]{2,1,0:T(8,128)(2,1)}, bf16[3,300,128]{2,1,0:T(8,128)(2,1)S(1)}, u32[]{:S(2)}, u32[]{:S(2)}) collective-permute-start(bf16[3,300,128]{2,1,0:T(8,128)(2,1)} %get-tuple-element.9), channel_id=1, source_target_pairs={{0,504},{8,0},{16,8},{24,16},{32,24},{40,32},{48,40},{56,48},{64,5... | collective-permute-start | bytes 691208 | tf_op jit(solution)/shard_map/ppermute | solution.py:226
  16.7 10.1 %all_to_all.15 = bf16[8,4,300]{2,1,0:T(4,128)(2,1)S(1)} all-to-all(bf16[8,4,300]{2,1,0:T(4,128)(2,1)} %get-tuple-element.8), channel_id=1, replica_groups=mesh['z'=16,'x'=4,'y'=4,'core'=2] {'y','core'}, dimensions={0} | all-to-all | bytes 38400 | tf_op jit(solution)/shard_map/all_to_all | solution.py:230
  26.9 0.0 collective-permute-done
  26.9 2.5 %all-gather = bf16[6,300,128]{2,1,0:T(8,128)(2,1)S(1)} all-gather(bf16[3,300,128]{2,1,0:T(8,128)(2,1)S(1)} %collective-permute-done), channel_id=2, replica_groups=mesh['z'=16,'x'=4,'y'=4,'core'=2] {'core'}, dimensions={0}, use_global_device_ids=true | all-gather | bytes 691200 | tf_op jit(solution)/shard_map/all_gather | solution.py:247
  29.4 0.0 copy-done
  29.4 0.0 copy-done.1
  29.4 0.0 copy-done.3
  29.4 0.0 copy-done.2
  29.4 7.5 %shard_map.69 = (bf16[300,32,128]{2,1,0:T(8,128)(2,1)S(1)}, bf16[16,2,40,128]{3,2,1,0:T(8,128)(2,1)S(1)}) custom-call(s32[8,128]{1,0:T(8,128)S(1)} %bitcast.10, f32[1,128]{1,0:T(1,128)S(1)} %bitcast.11, f32[24,24]{1,0:T(8,128)S(1)} %copy-done.1, bf16[32,300]{1,0:T(8,128)(2,1)S(1)} %reshape.18.coords_ref, bf16[3,300,1024]{2,1,0:T(8,128)(2,1)S(1)} %copy-done, ...), custom_call_target="tpu_custom_call" | custom-call | flops 7000000000 | bytes 5115392 | tf_op jit(solution)/shard_map/pallas_call | solution.py:209
  36.8 12.8 %all_to_all.16.arrived_ref = bf16[32,40,128]{2,1,0:T(8,128)(2,1)S(1)} all-to-all(bf16[32,40,128]{2,1,0:T(8,128)(2,1)S(1)} %bitcast.8), channel_id=1, replica_groups=mesh['z'=16,'x'=4,'y'=4,'core'=2] {'x','y','core'}, dimensions={0} | all-to-all | bytes 655360 | tf_op jit(solution)/shard_map/all_to_all | solution.py:230
  49.6 0.2 shard_map.70
  49.8 19.6 %all_to_all.17 = bf16[16,40,128]{2,1,0:T(8,128)(2,1)S(1)} all-to-all(bf16[16,40,128]{2,1,0:T(8,128)(2,1)S(1)} %shard_map.70), channel_id=1, replica_groups=mesh['z'=16,'x'=4,'y'=4,'core'=2] {'z'}, dimensions={0} | all-to-all | bytes 327680 | tf_op jit(solution)/shard_map/all_to_all | solution.py:230
  69.4 3.6 %all-gather.1 = f32[80,128]{1,0:T(8,128)S(1)} all-gather(f32[40,128]{1,0:T(8,128)S(1)} %convert_reduce_fusion), channel_id=3, replica_groups=mesh['z'=16,'x'=4,'y'=4,'core'=2] {'core'}, dimensions={0}, use_global_device_ids=true | all-gather | bytes 61440 | tf_op jit(solution)/shard_map/all_gather | solution.py:268
  73.0 2.4 %shard_map.71 = (bf16[300,32,128]{2,1,0:T(8,128)(2,1)}, f32[32,300]{1,0:T(8,128)}) custom-call(f32[2,40,128]{2,1,0:T(8,128)S(1)} %bitcast.9, bf16[300,32,128]{2,1,0:T(8,128)(2,1)S(1)} %get-tuple-element.11.columns_ref), custom_call_target="tpu_custom_call" | custom-call | bytes 4994560 | tf_op jit(solution)/shard_map/pallas_call | solution.py:209
  (2 shorter events, 0.0 us)
Async XLA Ops:
  0.6 28.7 %copy-start = (bf16[3,300,1024]{2,1,0:T(8,128)(2,1)S(1)}, bf16[3,300,1024]{2,1,0:T(8,128)(2,1)}, u32[]{:S(2)}) copy-start(bf16[3,300,1024]{2,1,0:T(8,128)(2,1)} %basis_ref.3) | copy-start | bytes 5529604
  0.6 28.7 %copy-start.1 = (f32[24,24]{1,0:T(8,128)S(1)}, f32[24,24]{1,0:T(8,128)}, u32[]{:S(2)}) copy-start(f32[24,24]{1,0:T(8,128)} %stiff_ref.1) | copy-start | bytes 6916
  0.7 28.7 %copy-start.3 = (f32[128]{0:T(128)S(1)}, f32[128]{0:T(128)}, u32[]{:S(2)}) copy-start(f32[128]{0:T(128)} %param.8) | copy-start | bytes 1540
  0.7 28.7 %copy-start.2 = (s32[128,8]{0,1:T(8,128)S(1)}, s32[128,8]{0,1:T(8,128)}, u32[]{:S(2)}) copy-start(s32[128,8]{0,1:T(8,128)} %param.7) | copy-start | bytes 12292
  2.6 24.3 %collective-permute-start = (bf16[3,300,128]{2,1,0:T(8,128)(2,1)}, bf16[3,300,128]{2,1,0:T(8,128)(2,1)S(1)}, u32[]{:S(2)}, u32[]{:S(2)}) collective-permute-start(bf16[3,300,128]{2,1,0:T(8,128)(2,1)} %get-tuple-element.9), channel_id=1, source_target_pairs={{0,504},{8,0},{16,8},{24,16},{32,24},{40,32},{48,40},{56,48},{64,5... | collective-permute-start | bytes 691208 | tf_op jit(solution)/shard_map/ppermute | solution.py:226

commit v3 on v2

--- a/solution.py
+++ b/solution.py
@@ -10,6 +10,7 @@
 VMEM = pl.BlockSpec(memory_space=pltpu.VMEM)
 ANY = pl.BlockSpec(memory_space=pl.ANY)
 DMA = pltpu.SemaphoreType.DMA
+EARLY = 2
 PITCH = 40
 ELEMS = 65536.0
 
@@ -75,10 +76,19 @@
     return dot(g_ref[group], r_ref[...])
 
 
+def local_body(conn_ref, basis_ref, *part_refs):
+    ids = corner_rows(conn_ref[...], lane_quarter())
+    for group, part_ref in enumerate(part_refs):
+        hot = (iota((basis_ref.shape[2], 256), 0) == ids[group]).astype(f32).astype(bf16)
+        for k in range(3):
+            part_ref[:, k * 256 : (k + 1) * 256] = dot(basis_ref[k], hot).astype(bf16)
+
+
 def stats_body(
-    conn_ref, mod_ref, stiff_ref, coords_ref, basis_ref, ghost_ref,
-    columns_ref, sums_ref, g_ref, x_ref, w_ref, r_ref, d_ref, acc_ref, wide_ref,
+    conn_ref, mod_ref, stiff_ref, coords_ref, basis_ref, ghost_ref, *refs
 ):
+    parts = refs[:EARLY]
+    columns_ref, sums_ref, g_ref, x_ref, w_ref, r_ref, d_ref, acc_ref, wide_ref = refs[EARLY:]
     quarter = lane_quarter()
     wide, diagonal = own_element(768), own_element(256)
     stiff = stiff_ref[...]
@@ -92,13 +102,19 @@
     ids = corner_rows(conn_ref[...], quarter)
     modes, nodes = basis_ref.shape[1:]
     for group in range(4):
-        hot = (iota((nodes, 256), 0) == ids[group]).astype(f32).astype(bf16)
+        if group >= EARLY:
+            hot = (iota((nodes, 256), 0) == ids[group]).astype(f32).astype(bf16)
         hot_ghost = (iota((256, 256), 0) + nodes == ids[group]).astype(f32).astype(bf16)
         for k in range(3):
             ghost = jnp.concatenate([ghost_ref[0, k], ghost_ref[1, k]], axis=1)
-            rows = dot(basis_ref[k], hot) + dot(ghost, hot_ghost)
-            g_ref[group, :, k * 256 : (k + 1) * 256] = rows.astype(bf16)
-    coords = coords_ref[...]
+            at = slice(k * 256, (k + 1) * 256)
+            rows = dot(ghost, hot_ghost)
+            if group >= EARLY:
+                g_ref[group, :, at] = (rows + dot(basis_ref[k], hot)).astype(bf16)
+            else:
+                g_ref[group, :, at] = rows.astype(bf16) + parts[group][:, at]
+    coords = jnp.concatenate([coords_ref[i].astype(f32) for i in range(coords_ref.shape[0])], axis=0)
+    coords = coords.astype(bf16)
     for group in range(4):
         d_ref[group * 32 : (group + 1) * 32, :] = dot(coords, g_ref[group]).astype(bf16)
     disp = d_ref[...]
@@ -240,16 +256,21 @@
         (DMA((11,)),),
         far=(1, 2),
         scalars=1,
+        flops=2 * 10**9,
         room=59,
     )
     ghost_half = passed_along(own_half, ("z", "x"), -1)
-    all_coords = exchanged(copies, ("y", "core")).reshape(-1, modes)
+    all_coords = exchanged(copies, ("y", "core"))
+    corner_ids = connectivity.T
+    parts = kernel(
+        local_body, (array((modes, 768), bf16),) * EARLY, (corner_ids, basis_rows), flops=2 * 10**9
+    )
     ghost = lax.all_gather(ghost_half, "core")
     rows_shape = (4, modes, 768)
     columns, sums = kernel(
         stats_body,
         (array((modes, 32, 128), bf16), array((16, 2, 40, 128), bf16)),
-        (connectivity.T, modulus.reshape(1, -1), stiffness, all_coords, basis_rows, ghost),
+        (corner_ids, modulus.reshape(1, -1), stiffness, all_coords, basis_rows, ghost, *parts),
         (
             pltpu.VMEM((4, modes, 768), bf16),
             pltpu.VMEM((4, 24, 8, 128), f32),
@@ -266,7 +287,7 @@
     (plane,) = kernel(middle_body, (array((16, 40, 128), bf16),), (plane,))
     half = exchanged(plane, "z").astype(f32).sum(axis=0)
     totals = lax.all_gather(half, "core")
-    step = 60
+    step = 30
     training, target = kernel(
         scaled_body,
         (array((modes, 32, 128), bf16), array((32, modes), f32)),

time: 75.7 us -> 74.8 us (0.988)
  blocking collectives: 48.5 us -> 40.6 us
  starting transfers between devices: 14.1 us -> 19.6 us
  waiting for transfers between devices: 0.01 us -> 1.27 us
    all_to_all x3 -> x2, blocking collectives: 42.5 us -> 34.9 us  [exchanged(): return lax.all_to_all(copies, axis, 0, 0, tiled=True)]
    all_to_all x0 -> x1, starting transfers between devices: none -> 5.43 us  [exchanged(): return lax.all_to_all(copies, axis, 0, 0, tiled=True)]
    all_to_all x0 -> x1, waiting for transfers between devices: none -> 1.27 us  [exchanged(): return lax.all_to_all(copies, axis, 0, 0, tiled=True)]
    pallas_call x4 -> x5, Pallas kernels: 11.9 us -> 12.3 us  [kernel(): pl.pallas_call(body, out_shape=out, in_specs=specs[:len(ins)], out_specs=...]
  transfers between devices with their start and end apart: 1 -> 2, of which waited for: 0 -> 1; matrix products, arithmetic and copies ran while one was open for 0% -> 0% of each run, Pallas kernels for 0% -> 2%
where the time goes in v3:
time: 74.8 us; the launch traced here: 74.5 us
  blocking collectives  40.6 us (54%)
  starting transfers between devices  19.6 us (26%)
  Pallas kernels  12.3 us (16%)
  waiting for transfers between devices  1.27 us (2%)
    all_to_all x2, blocking collectives, exchanged(): return lax.all_to_all(copies, axis, 0, 0, tiled=True)  34.9 us
    ppermute x1, starting transfers between devices, passed_along(): lax.ppermute(value, axis, [(i, (i + by) % peers) for i in range(peers)])  14.1 us
    pallas_call x5, Pallas kernels, kernel(): pl.pallas_call(body, out_shape=out, in_specs=specs[:len(ins)], out_specs=...  12.3 us
    all_to_all x1, starting transfers between devices, exchanged(): return lax.all_to_all(copies, axis, 0, 0, tiled=True)  5.43 us
    all_gather x1, blocking collectives, local(): totals = lax.all_gather(half, 'core')  3.58 us
    all_gather x1, blocking collectives, local(): ghost = lax.all_gather(ghost_half, 'core')  2.14 us
  transfers between devices with their start and end apart: 2, of which 1 were waited for; matrix products, arithmetic and copies ran while one was open for 0% of the time, Pallas kernels for 2%

profile of v3, /device:TPU:1, one launch (start us, length us, event | category | flops | bytes accessed | tf_op | source)
XLA Modules:
  0.0 74.5 jit_solution(1043981484732693894)
XLA Ops:
  0.6 0.0 copy-start
  0.6 0.0 copy-start.2
  0.7 1.9 %shard_map.68 = (bf16[3,300,128]{2,1,0:T(8,128)(2,1)}, bf16[8,4,300]{2,1,0:T(4,128)(2,1)}) custom-call(s32[1]{0:T(128)} %bitcast.2.core_ref, bf16[4,300]{1,0:T(4,128)(2,1)} %coords_ref.1, bf16[3,300,1024]{2,1,0:T(8,128)(2,1)} %basis_ref.5), custom_call_target="tpu_custom_call" | custom-call | flops 2000000000 | bytes 2095204 | tf_op jit(solution)/shard_map/pallas_call | solution.py:225
  2.6 14.1 %collective-permute-start = (bf16[3,300,128]{2,1,0:T(8,128)(2,1)}, bf16[3,300,128]{2,1,0:T(8,128)(2,1)S(1)}, u32[]{:S(2)}, u32[]{:S(2)}) collective-permute-start(bf16[3,300,128]{2,1,0:T(8,128)(2,1)} %get-tuple-element.11), channel_id=1, source_target_pairs={{0,504},{8,0},{16,8},{24,16},{32,24},{40,32},{48,40},{56,48},{64,5... | collective-permute-start | bytes 691208 | tf_op jit(solution)/shard_map/ppermute | solution.py:242
  16.7 5.4 %all-to-all-start = ((bf16[8,4,300]{2,1,0:T(4,128)(2,1)}), bf16[8,4,300]{2,1,0:T(4,128)(2,1)S(1)}, u32[]{:S(2)}, u32[]{:S(2)}) async-start(bf16[8,4,300]{2,1,0:T(4,128)(2,1)} %get-tuple-element.10), calls=%async_computation | async-start | bytes 49152 | tf_op jit(solution)/shard_map/all_to_all | solution.py:246
  22.1 0.0 copy-done
  22.2 0.0 copy-done.2
  22.2 0.0 copy-start.1
  22.2 0.0 copy-start.3
  22.2 1.2 %shard_map.69 = (bf16[300,768]{1,0:T(8,128)(2,1)S(1)}, bf16[300,768]{1,0:T(8,128)(2,1)S(1)}) custom-call(s32[8,128]{1,0:T(8,128)S(1)} %bitcast.10, bf16[3,300,1024]{2,1,0:T(8,128)(2,1)S(1)} %copy-done), custom_call_target="tpu_custom_call" | custom-call | flops 2000000000 | bytes 2768896 | tf_op jit(solution)/shard_map/pallas_call | solution.py:225
  23.4 0.0 collective-permute-done
  23.4 2.1 %all-gather = bf16[6,300,128]{2,1,0:T(8,128)(2,1)S(1)} all-gather(bf16[3,300,128]{2,1,0:T(8,128)(2,1)S(1)} %collective-permute-done), channel_id=2, replica_groups=mesh['z'=16,'x'=4,'y'=4,'core'=2] {'core'}, dimensions={0}, use_global_device_ids=true | all-gather | bytes 691200 | tf_op jit(solution)/shard_map/all_gather | solution.py:268
  25.6 1.3 %all-to-all-done.coords_ref = bf16[8,4,300]{2,1,0:T(4,128)(2,1)S(1)} async-done(((bf16[8,4,300]{2,1,0:T(4,128)(2,1)}), bf16[8,4,300]{2,1,0:T(4,128)(2,1)S(1)}, u32[]{:S(2)}, u32[]{:S(2)}) %all-to-all-start) | async-done | bytes 19232 | tf_op jit(solution)/shard_map/all_to_all | solution.py:246
  26.8 0.0 copy-done.1
  26.8 0.0 copy-done.3
  26.8 6.6 %shard_map.70 = (bf16[300,32,128]{2,1,0:T(8,128)(2,1)S(1)}, bf16[16,2,40,128]{3,2,1,0:T(8,128)(2,1)S(1)}) custom-call(s32[8,128]{1,0:T(8,128)S(1)} %bitcast.11, f32[1,128]{1,0:T(1,128)S(1)} %bitcast.12, f32[24,24]{1,0:T(8,128)S(1)} %copy-done.1, bf16[8,4,300]{2,1,0:T(4,128)(2,1)S(1)} %all-to-all-done.coords_ref, bf16[3,300,1024]{2,1,0:T(8,128)(2,1)S(1)} %copy-done, ...), custom_call_target="tpu_custom_call" | custom-call | flops 7000000000 | bytes 6036992 | tf_op jit(solution)/shard_map/pallas_call | solution.py:225
  33.4 13.1 %all_to_all.15.arrived_ref = bf16[32,40,128]{2,1,0:T(8,128)(2,1)S(1)} all-to-all(bf16[32,40,128]{2,1,0:T(8,128)(2,1)S(1)} %bitcast.8), channel_id=1, replica_groups=mesh['z'=16,'x'=4,'y'=4,'core'=2] {'x','y','core'}, dimensions={0} | all-to-all | bytes 655360 | tf_op jit(solution)/shard_map/all_to_all | solution.py:246
  46.5 0.2 shard_map.71
  46.7 21.8 %all_to_all.16 = bf16[16,40,128]{2,1,0:T(8,128)(2,1)S(1)} all-to-all(bf16[16,40,128]{2,1,0:T(8,128)(2,1)S(1)} %shard_map.71), channel_id=1, replica_groups=mesh['z'=16,'x'=4,'y'=4,'core'=2] {'z'}, dimensions={0} | all-to-all | bytes 327680 | tf_op jit(solution)/shard_map/all_to_all | solution.py:246
  68.5 3.6 %all-gather.1 = f32[80,128]{1,0:T(8,128)S(1)} all-gather(f32[40,128]{1,0:T(8,128)S(1)} %convert_reduce_fusion), channel_id=3, replica_groups=mesh['z'=16,'x'=4,'y'=4,'core'=2] {'core'}, dimensions={0}, use_global_device_ids=true | all-gather | bytes 61440 | tf_op jit(solution)/shard_map/all_gather | solution.py:289
  72.1 2.4 %shard_map.72 = (bf16[300,32,128]{2,1,0:T(8,128)(2,1)}, f32[32,300]{1,0:T(8,128)}) custom-call(f32[2,40,128]{2,1,0:T(8,128)S(1)} %bitcast.9, bf16[300,32,128]{2,1,0:T(8,128)(2,1)S(1)} %get-tuple-element.15.columns_ref), custom_call_target="tpu_custom_call" | custom-call | bytes 4994560 | tf_op jit(solution)/shard_map/pallas_call | solution.py:225
  (1 shorter events, 0.0 us)
Async XLA Ops:
  0.6 21.5 %copy-start = (bf16[3,300,1024]{2,1,0:T(8,128)(2,1)S(1)}, bf16[3,300,1024]{2,1,0:T(8,128)(2,1)}, u32[]{:S(2)}) copy-start(bf16[3,300,1024]{2,1,0:T(8,128)(2,1)} %basis_ref.5) | copy-start | bytes 5529604
  0.6 21.5 %copy-start.2 = (s32[128,8]{0,1:T(8,128)S(1)}, s32[128,8]{0,1:T(8,128)}, u32[]{:S(2)}) copy-start(s32[128,8]{0,1:T(8,128)} %param.7) | copy-start | bytes 12292
  2.6 20.9 %collective-permute-start = (bf16[3,300,128]{2,1,0:T(8,128)(2,1)}, bf16[3,300,128]{2,1,0:T(8,128)(2,1)S(1)}, u32[]{:S(2)}, u32[]{:S(2)}) collective-permute-start(bf16[3,300,128]{2,1,0:T(8,128)(2,1)} %get-tuple-element.11), channel_id=1, source_target_pairs={{0,504},{8,0},{16,8},{24,16},{32,24},{40,32},{48,40},{56,48},{64,5... | collective-permute-start | bytes 691208 | tf_op jit(solution)/shard_map/ppermute | solution.py:242
  16.7 10.1 %all-to-all-start = ((bf16[8,4,300]{2,1,0:T(4,128)(2,1)}), bf16[8,4,300]{2,1,0:T(4,128)(2,1)S(1)}, u32[]{:S(2)}, u32[]{:S(2)}) async-start(bf16[8,4,300]{2,1,0:T(4,128)(2,1)} %get-tuple-element.10), calls=%async_computation | async-start | bytes 49152 | tf_op jit(solution)/shard_map/all_to_all | solution.py:246
  22.2 4.7 %copy-start.1 = (f32[24,24]{1,0:T(8,128)S(1)}, f32[24,24]{1,0:T(8,128)}, u32[]{:S(2)}) copy-start(f32[24,24]{1,0:T(8,128)} %stiff_ref.1) | copy-start | bytes 6916
  22.2 4.7 %copy-start.3 = (f32[128]{0:T(128)S(1)}, f32[128]{0:T(128)}, u32[]{:S(2)}) copy-start(f32[128]{0:T(128)} %param.8) | copy-start | bytes 1540

commit v4 on v3

--- a/solution.py
+++ b/solution.py
@@ -57,14 +57,8 @@
     return (iota((32, lanes), 1) & 31) == iota((32, lanes), 0)
 
 
-def prepare_body(core_ref, coords_ref, basis_ref, half_ref, copies_ref, sem):
-    at = pl.ds(pl.multiple_of(core_ref[0] * 128, 128), 128)
-    loads = [pltpu.make_async_copy(basis_ref.at[k, :, at], half_ref.at[k], sem.at[k]) for k in range(3)]
-    loads += [pltpu.make_async_copy(coords_ref, copies_ref.at[i], sem.at[3 + i]) for i in range(8)]
-    for load in loads:
-        load.start()
-    for load in loads:
-        load.wait()
+def copies_body(coords_ref, copies_ref):
+    copies_ref[...] = jnp.broadcast_to(coords_ref[...][None], copies_ref.shape)
 
 
 def expanded_product(g_ref, x_ref, r_ref, group, pair, diagonal):
@@ -249,17 +243,9 @@
 def local(coords, basis_rows, connectivity, modulus, stiffness):
     modes = basis_rows.shape[1]
     core = lax.axis_index("core")
-    own_half, copies = kernel(
-        prepare_body,
-        (array((3, modes, 128), bf16), array((8, *coords.shape), bf16)),
-        (core.astype(jnp.int32).reshape(1), coords, basis_rows),
-        (DMA((11,)),),
-        far=(1, 2),
-        scalars=1,
-        flops=2 * 10**9,
-        room=59,
-    )
+    own_half = lax.dynamic_slice_in_dim(basis_rows, core * 128, 128, axis=2)
     ghost_half = passed_along(own_half, ("z", "x"), -1)
+    (copies,) = kernel(copies_body, (array((8, *coords.shape), bf16),), (coords,), flops=2 * 10**9)
     all_coords = exchanged(copies, ("y", "core"))
     corner_ids = connectivity.T
     parts = kernel(

time: 74.8 us -> 73.8 us (0.987)
  local copies, waits for them, and re-layouts: 0.02 us -> 1.67 us
  blocking collectives: 40.6 us -> 39.1 us
  Pallas kernels: 12.3 us -> 11 us
    all_to_all x2, blocking collectives: 34.9 us -> 33.4 us  [exchanged(): return lax.all_to_all(copies, axis, 0, 0, tiled=True)]
    pallas_call x5, Pallas kernels: 12.3 us -> 11 us  [kernel(): pl.pallas_call(body, out_shape=out, in_specs=specs[:len(ins)], out_specs=...]
    dynamic_slice x0 -> x1, local copies, waits for them, and re-layouts: none -> 0.96 us  [local(): own_half = lax.dynamic_slice_in_dim(basis_rows, core * 128, 128, axis=2)]
  transfers between devices with their start and end apart: 2 -> 2, of which waited for: 1 -> 1; matrix products, arithmetic and copies ran while one was open for 0% -> 0% of each run, Pallas kernels for 2% -> 3%
where the time goes in v4:
time: 73.8 us; the launch traced here: 73.5 us
  blocking collectives  39.1 us (53%)
  starting transfers between devices  19.7 us (27%)
  Pallas kernels  11 us (15%)
  local copies, waits for them, and re-layouts  1.67 us (2%)
  waiting for transfers between devices  1.27 us (2%)
    all_to_all x2, blocking collectives, exchanged(): return lax.all_to_all(copies, axis, 0, 0, tiled=True)  33.4 us
    ppermute x1, starting transfers between devices, passed_along(): lax.ppermute(value, axis, [(i, (i + by) % peers) for i in range(peers)])  14.3 us
    pallas_call x5, Pallas kernels, kernel(): pl.pallas_call(body, out_shape=out, in_specs=specs[:len(ins)], out_specs=...  11 us
    all_to_all x1, starting transfers between devices, exchanged(): return lax.all_to_all(copies, axis, 0, 0, tiled=True)  5.42 us
    all_gather x1, blocking collectives, local(): totals = lax.all_gather(half, 'core')  3.58 us
    all_gather x1, blocking collectives, local(): ghost = lax.all_gather(ghost_half, 'core')  2.14 us
  transfers between devices with their start and end apart: 2, of which 1 were waited for; matrix products, arithmetic and copies ran while one was open for 0% of the time, Pallas kernels for 3%

profile of v4, /device:TPU:1, one launch (start us, length us, event | category | flops | bytes accessed | tf_op | source)
XLA Modules:
  0.0 73.5 jit_solution(18264017589186746860)
XLA Ops:
  0.6 1.0 %constant_dynamic-slice_fusion = bf16[3,300,128]{2,1,0:T(8,128)(2,1)S(1)} fusion(bf16[3,300,1024]{2,1,0:T(8,128)(2,1)} %basis_ref.3, s32[]{:T(128)S(6)} %select_n.3), kind=kLoop, calls=%fused_computation.1 | loop fusion | bytes 460804 | tf_op jit(solution)/shard_map/dynamic_slice | solution.py:246
  1.6 0.0 copy-start
  1.6 0.0 copy-start.2
  1.6 14.3 %collective-permute-start = (bf16[3,300,128]{2,1,0:T(8,128)(2,1)S(1)}, bf16[3,300,128]{2,1,0:T(8,128)(2,1)S(1)}, u32[]{:S(2)}, u32[]{:S(2)}) collective-permute-start(bf16[3,300,128]{2,1,0:T(8,128)(2,1)S(1)} %constant_dynamic-slice_fusion), channel_id=1, source_target_pairs={{0,504},{8,0},{16,8},{24,16},{32,24},{40,32},{48,40},{56,48},{64,5... | collective-permute-start | bytes 691208 | tf_op jit(solution)/shard_map/ppermute | solution.py:236
  15.9 0.0 copy-start.3
  15.9 0.7 copy-done.3
  16.6 0.6 shard_map.68
  17.2 5.4 %all-to-all-start = ((bf16[8,4,300]{2,1,0:T(4,128)(2,1)}), bf16[8,4,300]{2,1,0:T(4,128)(2,1)S(1)}, u32[]{:S(2)}, u32[]{:S(2)}) async-start(bf16[8,4,300]{2,1,0:T(4,128)(2,1)} %shard_map.68), calls=%async_computation | async-start | bytes 49152 | tf_op jit(solution)/shard_map/all_to_all | solution.py:240
  22.6 0.0 copy-done
  22.6 0.0 copy-done.2
  22.6 0.0 copy-start.1
  22.6 0.0 copy-start.4
  22.7 1.2 %shard_map.69 = (bf16[300,768]{1,0:T(8,128)(2,1)S(1)}, bf16[300,768]{1,0:T(8,128)(2,1)S(1)}) custom-call(s32[8,128]{1,0:T(8,128)S(1)} %bitcast.9, bf16[3,300,1024]{2,1,0:T(8,128)(2,1)S(1)} %copy-done), custom_call_target="tpu_custom_call" | custom-call | flops 2000000000 | bytes 2768896 | tf_op jit(solution)/shard_map/pallas_call | solution.py:219
  23.9 0.0 collective-permute-done
  23.9 2.1 %all-gather = bf16[6,300,128]{2,1,0:T(8,128)(2,1)S(1)} all-gather(bf16[3,300,128]{2,1,0:T(8,128)(2,1)S(1)} %collective-permute-done), channel_id=2, replica_groups=mesh['z'=16,'x'=4,'y'=4,'core'=2] {'core'}, dimensions={0}, use_global_device_ids=true | all-gather | bytes 691200 | tf_op jit(solution)/shard_map/all_gather | solution.py:254
  26.1 1.3 %all-to-all-done.coords_ref = bf16[8,4,300]{2,1,0:T(4,128)(2,1)S(1)} async-done(((bf16[8,4,300]{2,1,0:T(4,128)(2,1)}), bf16[8,4,300]{2,1,0:T(4,128)(2,1)S(1)}, u32[]{:S(2)}, u32[]{:S(2)}) %all-to-all-start) | async-done | bytes 19232 | tf_op jit(solution)/shard_map/all_to_all | solution.py:240
  27.3 0.0 copy-done.1
  27.3 0.0 copy-done.4
  27.3 6.6 %shard_map.70 = (bf16[300,32,128]{2,1,0:T(8,128)(2,1)S(1)}, bf16[16,2,40,128]{3,2,1,0:T(8,128)(2,1)S(1)}) custom-call(s32[8,128]{1,0:T(8,128)S(1)} %bitcast.10, f32[1,128]{1,0:T(1,128)S(1)} %bitcast.11, f32[24,24]{1,0:T(8,128)S(1)} %copy-done.1, bf16[8,4,300]{2,1,0:T(4,128)(2,1)S(1)} %all-to-all-done.coords_ref, bf16[3,300,1024]{2,1,0:T(8,128)(2,1)S(1)} %copy-done, ...), custom_call_target="tpu_custom_call" | custom-call | flops 7000000000 | bytes 6036992 | tf_op jit(solution)/shard_map/pallas_call | solution.py:219
  33.9 13.1 %all_to_all.15.arrived_ref = bf16[32,40,128]{2,1,0:T(8,128)(2,1)S(1)} all-to-all(bf16[32,40,128]{2,1,0:T(8,128)(2,1)S(1)} %bitcast.7), channel_id=1, replica_groups=mesh['z'=16,'x'=4,'y'=4,'core'=2] {'x','y','core'}, dimensions={0} | all-to-all | bytes 655360 | tf_op jit(solution)/shard_map/all_to_all | solution.py:240
  47.0 0.2 shard_map.71
  47.2 20.3 %all_to_all.16 = bf16[16,40,128]{2,1,0:T(8,128)(2,1)S(1)} all-to-all(bf16[16,40,128]{2,1,0:T(8,128)(2,1)S(1)} %shard_map.71), channel_id=1, replica_groups=mesh['z'=16,'x'=4,'y'=4,'core'=2] {'z'}, dimensions={0} | all-to-all | bytes 327680 | tf_op jit(solution)/shard_map/all_to_all | solution.py:240
  67.5 3.6 %all-gather.1 = f32[80,128]{1,0:T(8,128)S(1)} all-gather(f32[40,128]{1,0:T(8,128)S(1)} %convert_reduce_fusion), channel_id=3, replica_groups=mesh['z'=16,'x'=4,'y'=4,'core'=2] {'core'}, dimensions={0}, use_global_device_ids=true | all-gather | bytes 61440 | tf_op jit(solution)/shard_map/all_gather | solution.py:275
  71.1 2.4 %shard_map.72 = (bf16[300,32,128]{2,1,0:T(8,128)(2,1)}, f32[32,300]{1,0:T(8,128)}) custom-call(f32[2,40,128]{2,1,0:T(8,128)S(1)} %bitcast.8, bf16[300,32,128]{2,1,0:T(8,128)(2,1)S(1)} %get-tuple-element.11.columns_ref), custom_call_target="tpu_custom_call" | custom-call | bytes 4994560 | tf_op jit(solution)/shard_map/pallas_call | solution.py:219
  (1 shorter events, 0.0 us)
Async XLA Ops:
  1.6 21.0 %copy-start = (bf16[3,300,1024]{2,1,0:T(8,128)(2,1)S(1)}, bf16[3,300,1024]{2,1,0:T(8,128)(2,1)}, u32[]{:S(2)}) copy-start(bf16[3,300,1024]{2,1,0:T(8,128)(2,1)} %basis_ref.3) | copy-start | bytes 5529604
  1.6 21.0 %copy-start.2 = (s32[128,8]{0,1:T(8,128)S(1)}, s32[128,8]{0,1:T(8,128)}, u32[]{:S(2)}) copy-start(s32[128,8]{0,1:T(8,128)} %param.7) | copy-start | bytes 12292
  1.6 22.3 %collective-permute-start = (bf16[3,300,128]{2,1,0:T(8,128)(2,1)S(1)}, bf16[3,300,128]{2,1,0:T(8,128)(2,1)S(1)}, u32[]{:S(2)}, u32[]{:S(2)}) collective-permute-start(bf16[3,300,128]{2,1,0:T(8,128)(2,1)S(1)} %constant_dynamic-slice_fusion), channel_id=1, source_target_pairs={{0,504},{8,0},{16,8},{24,16},{32,24},{40,32},{48,40},{56,48},{64,5... | collective-permute-start | bytes 691208 | tf_op jit(solution)/shard_map/ppermute | solution.py:236
  15.9 0.7 copy-start.3
  17.2 10.1 %all-to-all-start = ((bf16[8,4,300]{2,1,0:T(4,128)(2,1)}), bf16[8,4,300]{2,1,0:T(4,128)(2,1)S(1)}, u32[]{:S(2)}, u32[]{:S(2)}) async-start(bf16[8,4,300]{2,1,0:T(4,128)(2,1)} %shard_map.68), calls=%async_computation | async-start | bytes 49152 | tf_op jit(solution)/shard_map/all_to_all | solution.py:240
  22.6 4.7 %copy-start.1 = (f32[24,24]{1,0:T(8,128)S(1)}, f32[24,24]{1,0:T(8,128)}, u32[]{:S(2)}) copy-start(f32[24,24]{1,0:T(8,128)} %stiff_ref.1) | copy-start | bytes 6916
  22.6 4.7 %copy-start.4 = (f32[128]{0:T(128)S(1)}, f32[128]{0:T(128)}, u32[]{:S(2)}) copy-start(f32[128]{0:T(128)} %param.8) | copy-start | bytes 1540

commit v5 on v4

--- a/solution.py
+++ b/solution.py
@@ -57,8 +57,12 @@
     return (iota((32, lanes), 1) & 31) == iota((32, lanes), 0)
 
 
-def copies_body(coords_ref, copies_ref):
-    copies_ref[...] = jnp.broadcast_to(coords_ref[...][None], copies_ref.shape)
+def copies_body(coords_ref, copies_ref, sem):
+    copies = [pltpu.make_async_copy(coords_ref, copies_ref.at[i], sem.at[i]) for i in range(8)]
+    for copy in copies:
+        copy.start()
+    for copy in copies:
+        copy.wait()
 
 
 def expanded_product(g_ref, x_ref, r_ref, group, pair, diagonal):
@@ -245,7 +249,7 @@
     core = lax.axis_index("core")
     own_half = lax.dynamic_slice_in_dim(basis_rows, core * 128, 128, axis=2)
     ghost_half = passed_along(own_half, ("z", "x"), -1)
-    (copies,) = kernel(copies_body, (array((8, *coords.shape), bf16),), (coords,), flops=2 * 10**9)
+    (copies,) = kernel(copies_body, (array((8, *coords.shape), bf16),), (coords,), (DMA((8,)),), flops=2 * 10**9, far=(0, 1), room=60)
     all_coords = exchanged(copies, ("y", "core"))
     corner_ids = connectivity.T
     parts = kernel(

time: 73.8 us -> 73.8 us (level)
  Pallas kernels: 11 us -> 12.3 us
    pallas_call x5, Pallas kernels: 11 us -> 12.3 us  [kernel(): pl.pallas_call(body, out_shape=out, in_specs=specs[:len(ins)], out_specs=...]
  transfers between devices with their start and end apart: 2 -> 2, of which waited for: 1 -> 1; matrix products, arithmetic and copies ran while one was open for 0% -> 0% of each run, Pallas kernels for 3% -> 4%
where the time goes in v5:
time: 73.8 us; the launch traced here: 73.5 us
  blocking collectives  38.5 us (52%)
  starting transfers between devices  19.7 us (27%)
  Pallas kernels  12.3 us (17%)
  waiting for transfers between devices  1.27 us (2%)
  local copies, waits for them, and re-layouts  0.99 us (1%)
    all_to_all x2, blocking collectives, exchanged(): return lax.all_to_all(copies, axis, 0, 0, tiled=True)  32.7 us
    ppermute x1, starting transfers between devices, passed_along(): lax.ppermute(value, axis, [(i, (i + by) % peers) for i in range(peers)])  14.3 us
    pallas_call x5, Pallas kernels, kernel(): pl.pallas_call(body, out_shape=out, in_specs=specs[:len(ins)], out_specs=...  12.3 us
    all_to_all x1, starting transfers between devices, exchanged(): return lax.all_to_all(copies, axis, 0, 0, tiled=True)  5.43 us
    all_gather x1, blocking collectives, local(): totals = lax.all_gather(half, 'core')  3.58 us
    all_gather x1, blocking collectives, local(): ghost = lax.all_gather(ghost_half, 'core')  2.14 us
  transfers between devices with their start and end apart: 2, of which 1 were waited for; matrix products, arithmetic and copies ran while one was open for 0% of the time, Pallas kernels for 4%

profile of v5, /device:TPU:1, one launch (start us, length us, event | category | flops | bytes accessed | tf_op | source)
XLA Modules:
  0.0 73.5 jit_solution(5311632630111873168)
XLA Ops:
  0.6 1.0 %constant_dynamic-slice_fusion = bf16[3,300,128]{2,1,0:T(8,128)(2,1)S(1)} fusion(bf16[3,300,1024]{2,1,0:T(8,128)(2,1)} %basis_ref.3, s32[]{:T(128)S(6)} %select_n.3), kind=kLoop, calls=%fused_computation.1 | loop fusion | bytes 460804 | tf_op jit(solution)/shard_map/dynamic_slice | solution.py:250
  1.6 0.0 copy-start
  1.6 0.0 copy-start.2
  1.6 14.3 %collective-permute-start = (bf16[3,300,128]{2,1,0:T(8,128)(2,1)S(1)}, bf16[3,300,128]{2,1,0:T(8,128)(2,1)S(1)}, u32[]{:S(2)}, u32[]{:S(2)}) collective-permute-start(bf16[3,300,128]{2,1,0:T(8,128)(2,1)S(1)} %constant_dynamic-slice_fusion), channel_id=1, source_target_pairs={{0,504},{8,0},{16,8},{24,16},{32,24},{40,32},{48,40},{56,48},{64,5... | collective-permute-start | bytes 691208 | tf_op jit(solution)/shard_map/ppermute | solution.py:240
  15.9 1.9 %shard_map.68 = bf16[8,4,300]{2,1,0:T(4,128)(2,1)} custom-call(bf16[4,300]{1,0:T(4,128)(2,1)} %coords_ref.1), custom_call_target="tpu_custom_call" | custom-call | flops 2000000000 | bytes 21600 | tf_op jit(solution)/shard_map/pallas_call | solution.py:223
  17.8 5.4 %all-to-all-start = ((bf16[8,4,300]{2,1,0:T(4,128)(2,1)}), bf16[8,4,300]{2,1,0:T(4,128)(2,1)S(1)}, u32[]{:S(2)}, u32[]{:S(2)}) async-start(bf16[8,4,300]{2,1,0:T(4,128)(2,1)} %shard_map.68), calls=%async_computation | async-start | bytes 49152 | tf_op jit(solution)/shard_map/all_to_all | solution.py:244
  23.3 0.0 copy-done
  23.3 0.0 copy-done.2
  23.3 0.0 copy-start.1
  23.3 0.0 copy-start.3
  23.3 1.2 %shard_map.69 = (bf16[300,768]{1,0:T(8,128)(2,1)S(1)}, bf16[300,768]{1,0:T(8,128)(2,1)S(1)}) custom-call(s32[8,128]{1,0:T(8,128)S(1)} %bitcast.9, bf16[3,300,1024]{2,1,0:T(8,128)(2,1)S(1)} %copy-done), custom_call_target="tpu_custom_call" | custom-call | flops 2000000000 | bytes 2768896 | tf_op jit(solution)/shard_map/pallas_call | solution.py:223
  24.5 0.0 collective-permute-done
  24.6 2.1 %all-gather = bf16[6,300,128]{2,1,0:T(8,128)(2,1)S(1)} all-gather(bf16[3,300,128]{2,1,0:T(8,128)(2,1)S(1)} %collective-permute-done), channel_id=2, replica_groups=mesh['z'=16,'x'=4,'y'=4,'core'=2] {'core'}, dimensions={0}, use_global_device_ids=true | all-gather | bytes 691200 | tf_op jit(solution)/shard_map/all_gather | solution.py:258
  26.7 1.3 %all-to-all-done.coords_ref = bf16[8,4,300]{2,1,0:T(4,128)(2,1)S(1)} async-done(((bf16[8,4,300]{2,1,0:T(4,128)(2,1)}), bf16[8,4,300]{2,1,0:T(4,128)(2,1)S(1)}, u32[]{:S(2)}, u32[]{:S(2)}) %all-to-all-start) | async-done | bytes 19232 | tf_op jit(solution)/shard_map/all_to_all | solution.py:244
  28.0 0.0 copy-done.1
  28.0 0.0 copy-done.3
  28.0 6.6 %shard_map.70 = (bf16[300,32,128]{2,1,0:T(8,128)(2,1)S(1)}, bf16[16,2,40,128]{3,2,1,0:T(8,128)(2,1)S(1)}) custom-call(s32[8,128]{1,0:T(8,128)S(1)} %bitcast.10, f32[1,128]{1,0:T(1,128)S(1)} %bitcast.11, f32[24,24]{1,0:T(8,128)S(1)} %copy-done.1, bf16[8,4,300]{2,1,0:T(4,128)(2,1)S(1)} %all-to-all-done.coords_ref, bf16[3,300,1024]{2,1,0:T(8,128)(2,1)S(1)} %copy-done, ...), custom_call_target="tpu_custom_call" | custom-call | flops 7000000000 | bytes 6036992 | tf_op jit(solution)/shard_map/pallas_call | solution.py:223
  34.6 13.1 %all_to_all.15.arrived_ref = bf16[32,40,128]{2,1,0:T(8,128)(2,1)S(1)} all-to-all(bf16[32,40,128]{2,1,0:T(8,128)(2,1)S(1)} %bitcast.7), channel_id=1, replica_groups=mesh['z'=16,'x'=4,'y'=4,'core'=2] {'x','y','core'}, dimensions={0} | all-to-all | bytes 655360 | tf_op jit(solution)/shard_map/all_to_all | solution.py:244
  47.7 0.2 shard_map.71
  47.9 19.6 %all_to_all.16 = bf16[16,40,128]{2,1,0:T(8,128)(2,1)S(1)} all-to-all(bf16[16,40,128]{2,1,0:T(8,128)(2,1)S(1)} %shard_map.71), channel_id=1, replica_groups=mesh['z'=16,'x'=4,'y'=4,'core'=2] {'z'}, dimensions={0} | all-to-all | bytes 327680 | tf_op jit(solution)/shard_map/all_to_all | solution.py:244
  67.5 3.6 %all-gather.1 = f32[80,128]{1,0:T(8,128)S(1)} all-gather(f32[40,128]{1,0:T(8,128)S(1)} %convert_reduce_fusion), channel_id=3, replica_groups=mesh['z'=16,'x'=4,'y'=4,'core'=2] {'core'}, dimensions={0}, use_global_device_ids=true | all-gather | bytes 61440 | tf_op jit(solution)/shard_map/all_gather | solution.py:279
  71.1 2.4 %shard_map.72 = (bf16[300,32,128]{2,1,0:T(8,128)(2,1)}, f32[32,300]{1,0:T(8,128)}) custom-call(f32[2,40,128]{2,1,0:T(8,128)S(1)} %bitcast.8, bf16[300,32,128]{2,1,0:T(8,128)(2,1)S(1)} %get-tuple-element.11.columns_ref), custom_call_target="tpu_custom_call" | custom-call | bytes 4994560 | tf_op jit(solution)/shard_map/pallas_call | solution.py:223
  (1 shorter events, 0.0 us)
Async XLA Ops:
  1.6 21.7 %copy-start = (bf16[3,300,1024]{2,1,0:T(8,128)(2,1)S(1)}, bf16[3,300,1024]{2,1,0:T(8,128)(2,1)}, u32[]{:S(2)}) copy-start(bf16[3,300,1024]{2,1,0:T(8,128)(2,1)} %basis_ref.3) | copy-start | bytes 5529604
  1.6 21.7 %copy-start.2 = (s32[128,8]{0,1:T(8,128)S(1)}, s32[128,8]{0,1:T(8,128)}, u32[]{:S(2)}) copy-start(s32[128,8]{0,1:T(8,128)} %param.7) | copy-start | bytes 12292
  1.6 22.9 %collective-permute-start = (bf16[3,300,128]{2,1,0:T(8,128)(2,1)S(1)}, bf16[3,300,128]{2,1,0:T(8,128)(2,1)S(1)}, u32[]{:S(2)}, u32[]{:S(2)}) collective-permute-start(bf16[3,300,128]{2,1,0:T(8,128)(2,1)S(1)} %constant_dynamic-slice_fusion), channel_id=1, source_target_pairs={{0,504},{8,0},{16,8},{24,16},{32,24},{40,32},{48,40},{56,48},{64,5... | collective-permute-start | bytes 691208 | tf_op jit(solution)/shard_map/ppermute | solution.py:240
  17.8 10.1 %all-to-all-start = ((bf16[8,4,300]{2,1,0:T(4,128)(2,1)}), bf16[8,4,300]{2,1,0:T(4,128)(2,1)S(1)}, u32[]{:S(2)}, u32[]{:S(2)}) async-start(bf16[8,4,300]{2,1,0:T(4,128)(2,1)} %shard_map.68), calls=%async_computation | async-start | bytes 49152 | tf_op jit(solution)/shard_map/all_to_all | solution.py:244
  23.3 4.7 %copy-start.1 = (f32[24,24]{1,0:T(8,128)S(1)}, f32[24,24]{1,0:T(8,128)}, u32[]{:S(2)}) copy-start(f32[24,24]{1,0:T(8,128)} %stiff_ref.1) | copy-start | bytes 6916
  23.3 4.7 %copy-start.3 = (f32[128]{0:T(128)S(1)}, f32[128]{0:T(128)}, u32[]{:S(2)}) copy-start(f32[128]{0:T(128)} %param.8) | copy-start | bytes 1540
